TPU v7x, 256 devices: a whole 4x4x8 slice. The times are simulated.
256 devices in a mesh: ctx: 64 (over x, z, core), head: 4 (over y).
Axes of the slice: x: 4, y: 4, z: 8, core: 2. Of those that a mesh axis runs over, the one named last changes fastest.
Arguments:
- queries: bfloat16 [16384, 2560], P('ctx', 'head'), may hold values from -8 to 8
- key_tokens: bfloat16 [16384, 2560], P('ctx', 'head'), may hold values from -8 to 8
- value_tokens: bfloat16 [16384, 2560], P('ctx', 'head'), may hold values from -8 to 8
- pair_keys: int32 [512, 4], P('ctx'), may hold values from 0 to 511, as said below
- pair_count: int32 [512], P('ctx'), may hold values from 1 to 4, as said below
Outputs:
- attended: bfloat16 [16384, 2560], P('ctx', 'head')
Inputs may be any that keep to these rules, and one draw needn't show every extreme that they name: `pair_keys`: the 4 entries of a row are distinct, padded slots too. Key block c lies on index c // 8 of ctx. Among all 4 slots (padded ones included) of the 8 rows of one index of ctx, at most 2 name key blocks of any one index, its own included, and on every index some one index is named exactly 2 times. `pair_count`: every index of ctx has a query block whose count is 4.
All inputs are finite; a program needn't handle non-finite values.
Results may differ from a plain program's by a relative error of at most 0.0059.
Values may be sent and summed in bfloat16 or wider, within the bound.
No kernel may reach another device: no remote copies, remote signals or barrier semaphores. Data moves between devices by JAX's collectives and lax.ppermute only.
A program may use at most 128 MiB of HBM per device.

v0:
```python
import functools
import math

import jax
import jax.numpy as jnp
from jax import lax
from jax.experimental import pallas as pl
from jax.experimental.pallas import tpu as pltpu
from jax.sharding import PartitionSpec as P

HD = 128
BLOCK = 32
NX, NZ, NC = 4, 8, 2
BLOCKS = 8
SLOTS = 4
TOKENS = BLOCKS * BLOCK
HALF = TOKENS // 2
REQUEST = 16
STATS = 32
MEANS = 16
PLANE = NX * NC
MOST = 2 * PLANE
FIRST = 2
CHUNK = 4
NEGATIVE = -1e30
ROWS_ROWS = (((1,), (1,)), ((), ()))
COLS_COLS = (((0,), (0,)), ((), ()))
PARAMS = pltpu.CompilerParams(vmem_limit_bytes=10 * 1024 * 1024)


def move(array, dx=0, dz=0, dc=0):
    pairs = []
    for x in range(NX):
        for z in range(NZ):
            for c in range(NC):
                to = (((x + dx) % NX) * NZ + (z + dz) % NZ) * NC + (c ^ dc)
                pairs.append(((x * NZ + z) * NC + c, to))
    return lax.ppermute(array, "ctx", pairs)


def iota(shape, axis):
    return lax.broadcasted_iota(jnp.int32, shape, axis)


ENTRY = 32
MEAN_KEYS = PLANE * BLOCKS


def list_kernel(first, spec, pos_ref, asked_ref, bias_ref, list_ref, ids_vmem, ids_ref, sem):
    mx, mz, mc = pos_ref[0], pos_ref[1], pos_ref[2]
    tables = ids_vmem.shape[0]
    row = iota((BLOCKS, HD), 0)
    for table in range(tables):
        rows = pl.ds(first + table * REQUEST, REQUEST)
        request = asked_ref[rows, :HD].astype(jnp.float32)
        owner, within = request[:BLOCKS].astype(jnp.int32), request[BLOCKS:].astype(jnp.int32)
        here = (owner >= 0) & (((owner >> 1) & (NZ - 1)) == mz)
        rel = (((owner >> 4) - mx) & (NX - 1)) * NC + ((owner & 1) ^ mc)
        ids_vmem[table] = jnp.where(here, (row * PLANE + rel) * BLOCKS + within, -1)
    ids_copy = pltpu.make_async_copy(ids_vmem, ids_ref, sem)
    ids_copy.start()
    ids_copy.wait()

    for g, (table, low, high) in enumerate(spec):

        def ask(b, n, g=g, table=table):
            for p in range(SLOTS):
                code = ids_ref[table, b, p]
                list_ref[g, ENTRY + n] = code
                n = n + (code >= 0).astype(jnp.int32)
            return n

        used = lax.fori_loop(low, high, ask, jnp.int32(0))
        list_ref[g, 0] = used

        def blank(n, carry, g=g):
            list_ref[g, ENTRY + n] = -1
            return carry

        lax.fori_loop(used, FIRST + MOST, blank, 0)

    shape = (MEAN_KEYS, TOKENS)
    key_ids, token_blocks = iota(shape, 0), iota(shape, 1) // BLOCK
    for table in range(tables):
        bias = jnp.full(shape, math.log(BLOCK), jnp.float32)
        for g in range(len(spec)):
            if spec[g][0] != table:
                continue

            def exclude(n, bias, g=g):
                code = list_ref[g, ENTRY + n]
                hit = (key_ids == (code & (MEAN_KEYS - 1))) & (token_blocks == code >> 6)
                return jnp.where(hit, NEGATIVE, bias)

            bias = lax.fori_loop(0, list_ref[g, 0], exclude, bias)
        bias_ref[table] = bias


def make_lists(position, asked, first, tables, spec):
    vmem = pl.BlockSpec(memory_space=pltpu.VMEM)
    smem = pl.BlockSpec(memory_space=pltpu.SMEM)
    return pl.pallas_call(
        functools.partial(list_kernel, first, spec),
        in_specs=[smem, vmem],
        out_specs=[vmem, smem],
        out_shape=[
            jax.ShapeDtypeStruct((tables, MEAN_KEYS, TOKENS), jnp.float32),
            jax.ShapeDtypeStruct((len(spec), HD), jnp.int32),
        ],
        scratch_shapes=[
            pltpu.VMEM((tables, BLOCKS, HD), jnp.int32),
            pltpu.SMEM((tables, BLOCKS, HD), jnp.int32),
            pltpu.SemaphoreType.DMA,
        ],
        compiler_params=PARAMS,
        cost_estimate=pl.CostEstimate(flops=1000000, bytes_accessed=1024 * 1024, transcendentals=0),
    )(position, asked)


def means_kernel(*refs):
    sources, (mean_k_ref, mean_v_ref) = refs[:PLANE], refs[PLANE:]
    tiles = [source[TOKENS : TOKENS + MEANS].astype(jnp.float32) for source in sources]
    mean_k_ref[...] = jnp.concatenate([t[:BLOCKS] for t in tiles], axis=0).astype(jnp.bfloat16)
    mean_v_ref[...] = jnp.concatenate([t[BLOCKS:] for t in tiles], axis=0).astype(jnp.bfloat16)


def gather_means(sources):
    shape = jax.ShapeDtypeStruct((MEAN_KEYS, sources[0].shape[1]), jnp.bfloat16)
    return pl.pallas_call(
        means_kernel,
        out_shape=(shape, shape),
        compiler_params=PARAMS,
        cost_estimate=pl.CostEstimate(flops=1000000, bytes_accessed=1024 * 1024, transcendentals=0),
    )(*sources)


def own_kernel(key_ref, value_ref, out_ref, sem):
    split = TOKENS + MEANS
    starts = (0, split)
    copies = []
    for n, ref in enumerate((key_ref, value_ref)):
        target = out_ref.at[pl.ds(starts[n], TOKENS)]
        copies.append(pltpu.make_async_copy(ref, target, sem.at[n]))
        copies[n].start()
    means = []
    for first, copy in zip(starts, copies):
        copy.wait()
        for b in range(BLOCKS):
            rows = pl.ds(first + b * BLOCK, BLOCK)
            block = out_ref[rows].astype(jnp.float32)
            means.append(jnp.sum(block, axis=0, keepdims=True) * (1.0 / BLOCK))
    out_ref[TOKENS:split] = jnp.concatenate(means, axis=0).astype(jnp.bfloat16)


def make_own(keys, values):
    rows = 2 * TOKENS + MEANS
    return pl.pallas_call(
        own_kernel,
        in_specs=[pl.BlockSpec(memory_space=pl.ANY)] * 2,
        out_shape=jax.ShapeDtypeStruct((rows, keys.shape[1]), jnp.bfloat16),
        scratch_shapes=[pltpu.SemaphoreType.DMA((2,))],
        compiler_params=PARAMS,
    )(keys, values)


def part_kernel(heads, groups, list_ref, mean_k_ref, mean_v_ref, bias_ref, *rest):
    count = len(groups)
    key_refs, rest = rest[:PLANE], rest[PLANE:]
    value_refs, rest = rest[:PLANE], rest[PLANE:]
    q_refs, rest = rest[:count], rest[count:]
    out_refs, rest = rest[:count], rest[count:]
    accs, rest = rest[:count], rest[count:]
    tops, rest = rest[:count], rest[count:]
    sums, bufs = rest[:count], rest[count:]
    inv_root = 1.0 / math.sqrt(HD)
    chunks = []
    for g in range(count):
        which = groups[g][3]
        used = list_ref[which, 0]
        chunks.append((jnp.maximum(used - FIRST, 0) + CHUNK - 1) // CHUNK)

        def fetch(n, carry, g=g, which=which):
            key = list_ref[which, ENTRY + n] & (MEAN_KEYS - 1)
            first = pl.multiple_of((key % BLOCKS) * BLOCK, BLOCK)
            for i in range(PLANE):

                @pl.when(key // BLOCKS == i)
                def _(i=i):
                    skip = value_refs[i].shape[0] - TOKENS
                    rows = pl.ds(pl.multiple_of(first + skip, 16), BLOCK)
                    bufs[g][n, :BLOCK] = key_refs[i][pl.ds(first, BLOCK)]
                    bufs[g][n, BLOCK:] = value_refs[i][rows]

            return carry

        lax.fori_loop(0, FIRST + CHUNK * chunks[g], fetch, 0)

    def slots_of(g, first, number):
        _, low, blocks, which, _ = groups[g]
        token_blocks = iota((1, blocks * BLOCK), 1) // BLOCK + low
        places, rows = [], []
        for j in range(number):
            code = list_ref[which, ENTRY + first + j]
            places.append((g, first + j))
            rows.append(jnp.where(token_blocks == code >> 6, 0.0, NEGATIVE))
        return places, rows

    def keys_of(places, cols):
        return [bufs[g][n, :BLOCK, cols] for g, n in places]

    def values_of(places, cols):
        return [bufs[g][n, BLOCK:, cols] for g, n in places]

    def logits_of(g, keys, cols, biases):
        pieces = [q_refs[g][row : row + HALF, cols] for row in groups[g][0]]
        queries = pieces[0] if len(pieces) == 1 else jnp.concatenate(pieces, axis=0)
        logits = lax.dot_general(
            jnp.concatenate(keys, axis=0), queries, ROWS_ROWS, preferred_element_type=jnp.float32
        )
        logits = logits * inv_root
        pieces, row = [], 0
        for key, bias in zip(keys, biases):
            pieces.append(logits[row : row + key.shape[0]] + bias)
            row += key.shape[0]
        return jnp.concatenate(pieces, axis=0)

    def summed(values, weights):
        return lax.dot_general(
            jnp.concatenate(values, axis=0),
            weights,
            COLS_COLS,
            preferred_element_type=jnp.float32,
        )

    all_cols = [pl.ds(h * HD, HD) for h in range(heads)]
    for g in range(count):
        _, low, blocks, _, table = groups[g]
        places, rows = slots_of(g, 0, FIRST)
        bias = bias_ref[table, :, low * BLOCK : (low + blocks) * BLOCK]
        tiles = [
            logits_of(g, [mean_k_ref[:, cols]] + keys_of(places, cols), cols, [bias] + rows)
            for cols in all_cols
        ]
        for h, cols in enumerate(all_cols):
            top = jnp.max(tiles[h], axis=0, keepdims=True)
            weights = jnp.exp(tiles[h] - top)
            tops[g][h : h + 1] = top
            sums[g][h : h + 1] = jnp.sum(weights, axis=0, keepdims=True)
            tiles[h] = weights.astype(jnp.bfloat16)
        for h, cols in enumerate(all_cols):
            accs[g][cols] = summed([mean_v_ref[:, cols]] + values_of(places, cols), tiles[h])

    for g in range(count):

        def chunk(ci, carry, g=g):
            places, rows = slots_of(g, FIRST + ci * CHUNK, CHUNK)
            tiles = [logits_of(g, keys_of(places, cols), cols, rows) for cols in all_cols]
            ratios = []
            for h in range(heads):
                before = tops[g][h : h + 1]
                top = jnp.maximum(before, jnp.max(tiles[h], axis=0, keepdims=True))
                weights = jnp.exp(tiles[h] - top)
                ratio = jnp.exp(before - top)
                tops[g][h : h + 1] = top
                sums[g][h : h + 1] = sums[g][h : h + 1] * ratio + jnp.sum(
                    weights, axis=0, keepdims=True
                )
                tiles[h] = weights.astype(jnp.bfloat16)
                ratios.append(ratio)
            for h, cols in enumerate(all_cols):
                accs[g][cols] = accs[g][cols] * ratios[h] + summed(
                    values_of(places, cols), tiles[h]
                )
            return carry

        lax.fori_loop(0, chunks[g], chunk, 0)

    for g in range(count):
        top = tops[g][...]
        sent = top.astype(jnp.bfloat16).astype(jnp.float32)
        factor = jnp.exp(top - sent)
        for h, cols in enumerate(all_cols):
            out_refs[g][cols] = (accs[g][cols] * factor[h : h + 1]).astype(jnp.bfloat16)
        write_stats(out_refs[g], slice(None), heads, sent, sums[g][...] * factor)


def write_stats(out_ref, lanes, heads, top, total):
    high = total.astype(jnp.bfloat16).astype(jnp.float32)
    rows = (top, high, total - high, jnp.zeros_like(top))
    valid = iota(top.shape, 0) < heads
    rows = [jnp.where(valid, r, 0.0) for r in rows]
    out_ref[heads * HD :, lanes] = jnp.concatenate(rows, axis=0).astype(jnp.bfloat16)


def part(plane, bias, lists, queries, groups):
    columns = queries[0].shape[1]
    heads = columns // HD
    vmem = pl.BlockSpec(memory_space=pltpu.VMEM)
    smem = pl.BlockSpec(memory_space=pltpu.SMEM)
    widths = [group[2] * BLOCK for group in groups]
    scratch = [pltpu.VMEM((columns, w), jnp.float32) for w in widths]
    scratch += [pltpu.VMEM((8, w), jnp.float32) for w in widths] * 2
    scratch += [pltpu.VMEM((FIRST + MOST, 2 * BLOCK, columns), jnp.bfloat16) for _ in widths]
    mean_k, mean_v, key_refs, value_refs = plane
    operands = (mean_k, mean_v, bias, *key_refs, *value_refs, *queries)
    return pl.pallas_call(
        functools.partial(part_kernel, heads, groups),
        in_specs=[smem] + [vmem] * len(operands),
        out_specs=[vmem] * len(groups),
        out_shape=[jax.ShapeDtypeStruct((columns + STATS, w), jnp.bfloat16) for w in widths],
        scratch_shapes=scratch,
        compiler_params=PARAMS,
        cost_estimate=pl.CostEstimate(
            flops=4 * 512 * 1024 * columns, bytes_accessed=4 * 1024 * 1024, transcendentals=500000
        ),
    )(lists, *operands)


def stats_of(ref, lanes, heads):
    rows = ref[heads * HD :, lanes].astype(jnp.float32)
    return rows[:8], rows[8:16] + rows[16:24]


def merged(heads, parts):
    stats = [stats_of(ref, lanes, heads) for ref, lanes in parts]
    top = functools.reduce(jnp.maximum, [s[0] for s in stats])
    ratios = [jnp.exp(s[0] - top) for s in stats]
    total = functools.reduce(jnp.add, [r * s[1] for r, s in zip(ratios, stats)])
    return top, ratios, total


def merge_kernel(heads, up_ref, up_in_ref, down_ref, down_in_ref, up_out, down_out):
    for own, came, out, up in (
        (up_ref, up_in_ref, up_out, True),
        (down_ref, down_in_ref, down_out, False),
    ):
        width = came.shape[1]
        if width == own.shape[1]:
            lanes = slice(None)
        else:
            lanes = slice(0, width) if up else slice(width, 2 * width)
            rest = slice(width, 2 * width) if up else slice(0, width)
            out[:, rest] = own[:, rest]
        top, ratios, total = merged(heads, ((own, lanes), (came, slice(None))))
        for h in range(heads):
            cols = pl.ds(h * HD, HD)
            one = own[cols, lanes].astype(jnp.float32) * ratios[0][h : h + 1]
            two = came[cols, :].astype(jnp.float32) * ratios[1][h : h + 1]
            out[cols, lanes] = (one + two).astype(jnp.bfloat16)
        write_stats(out, lanes, heads, top, total)


def merge(up, up_in, down, down_in):
    heads = (up.shape[0] - STATS) // HD
    whole = jax.ShapeDtypeStruct(up.shape, jnp.bfloat16)
    return pl.pallas_call(
        functools.partial(merge_kernel, heads),
        out_shape=(whole, whole),
        compiler_params=PARAMS,
        cost_estimate=pl.CostEstimate(
            flops=1000000, bytes_accessed=2 * 1024 * 1024, transcendentals=1000
        ),
    )(up, up_in, down, down_in)


def last_kernel(heads, own_ref, up_ref, down_ref, out_ref):
    refs = (own_ref, up_ref, down_ref)
    _, ratios, total = merged(heads, [(ref, slice(None)) for ref in refs])
    valid = iota(total.shape, 0) < heads
    scales = [r / jnp.where(valid, total, 1.0) for r in ratios]
    for h in range(heads):
        cols = pl.ds(h * HD, HD)
        whole = jnp.zeros((HD, TOKENS), jnp.float32)
        for ref, scale in zip(refs, scales):
            whole = whole + ref[cols].astype(jnp.float32) * scale[h : h + 1]
        out_ref[:, cols] = jnp.transpose(whole).astype(out_ref.dtype)


def last(own, up, down):
    columns = own.shape[0] - STATS
    return pl.pallas_call(
        functools.partial(last_kernel, columns // HD),
        out_shape=jax.ShapeDtypeStruct((TOKENS, columns), jnp.bfloat16),
        compiler_params=PARAMS,
    )(own, up, down)


def body(queries, key_tokens, value_tokens, pair_keys, pair_count):
    tok_rows, columns = queries.shape
    assert lax.axis_size("ctx") == NX * NZ * NC
    assert tok_rows == TOKENS and pair_keys.shape == (BLOCKS, SLOTS)
    me = lax.axis_index("ctx")
    position = jnp.stack((me // (NZ * NC), (me // NC) % NZ, me % NC)).astype(jnp.int32)
    barrier = lax.optimization_barrier

    usable = jnp.arange(SLOTS, dtype=jnp.int32)[None, :] < pair_count[:, None]
    asked = jnp.concatenate(
        (jnp.where(usable, pair_keys // BLOCKS, -1), pair_keys % BLOCKS), axis=0
    ).astype(jnp.bfloat16)
    asked = jnp.pad(asked, ((0, 0), (0, columns - SLOTS)))
    pay = jnp.concatenate((queries[:HALF], asked, queries[HALF:]), axis=0)

    split = TOKENS + MEANS
    def means(tokens):
        grouped = tokens.reshape(BLOCKS, BLOCK, columns).astype(jnp.float32)
        return jnp.mean(grouped, axis=1).astype(jnp.bfloat16)

    own = jnp.concatenate(
        (key_tokens, means(key_tokens), means(value_tokens), value_tokens), axis=0
    )
    up1, down1 = move(pay, dz=1), move(pay, dz=-1)
    left, right = move(own, dx=1), move(own, dx=-1)
    own_twin = move(own, dc=1)
    up2, down2 = move(up1, dz=1), move(down1, dz=-1)
    far_k, far_v = move(left[:split], dx=1), move(right[split:], dx=-1)
    left_twin, right_twin = move(left, dc=1), move(right, dc=1)
    up3, down3 = move(up2, dz=1), move(down2, dz=-1)
    far_k_twin, far_v_twin = move(far_k, dc=1), move(far_v, dc=1)
    far_up = move(up3[: HALF + REQUEST], dz=1)
    far_down = move(down3[HALF:], dz=-1)
    far_up, far_down = barrier((far_up, far_down))
    key_refs = (own, own_twin, right, right_twin, far_k, far_k_twin, left, left_twin)
    value_refs = (own, own_twin, right, right_twin, far_v, far_v_twin, left, left_twin)
    plane = (*gather_means(key_refs), key_refs, value_refs)
    payloads = (pay, up1, down1, up2, down2, up3, down3)
    requests = [p[HALF : HALF + REQUEST, :HD] for p in payloads]
    tables = len(payloads)
    near = make_lists(
        position,
        jnp.concatenate(requests, axis=0),
        0,
        tables,
        tuple((table, 0, BLOCKS) for table in range(tables)),
    )
    both, mid = (0, HALF + REQUEST), BLOCKS // 2
    far = make_lists(position, far_up, HALF, 1, ((0, 0, mid), (0, mid, BLOCKS)))

    up_in, down_in = part(
        plane, *far, (far_up, far_down), (((0,), 0, mid, 0, 0), ((REQUEST,), mid, mid, 1, 0))
    )
    up_in, down_in = move(up_in, dz=-1), move(down_in, dz=1)
    for hop, up, down in ((3, up3, down3), (2, up2, down2), (1, up1, down1)):
        first = 2 * hop - 1
        groups = tuple((both, 0, BLOCKS, first + i, first + i) for i in range(2))
        up_part, down_part = part(plane, *near, (up, down), groups)
        up_sum, down_sum = merge(up_part, up_in, down_part, down_in)
        up_in, down_in = move(up_sum, dz=-1), move(down_sum, dz=1)
    (own_part,) = part(plane, *near, (pay,), ((both, 0, BLOCKS, 0, 0),))
    return last(own_part, up_in, down_in)


def solution(mesh):
    placed = (P("ctx", "head"), P("ctx", "head"), P("ctx", "head"), P("ctx", None), P("ctx"))
    return jax.shard_map(
        body, mesh=mesh, in_specs=placed, out_specs=P("ctx", "head"), check_vma=False
    )
```

profile of v0, /device:TPU:6, one launch (start us, length us, event | category | flops | bytes accessed | tf_op | source)
XLA Modules:
  0.0 98.7 jit_solution(13203988986095792677)
XLA Ops:
  0.0 0.7 fusion.1
  0.7 0.1 pad_maximum_fusion.2
  0.8 0.1 copy.10
  0.9 1.1 %fusion.4 = (bf16[128,640]{1,0:T(8,128)(2,1)S(1)}, bf16[128,640]{1,0:T(8,128)(2,1)S(1)}) fusion(bf16[256,640]{1,0:T(8,128)(2,1)} %param.5), kind=kLoop, calls=%fused_computation.28 | loop fusion | bytes 655360 | tf_op jit(solution)/shard_map/slice | solution.py:401
  2.0 0.0 copy-start.1
  2.0 2.0 %collective-permute-start = (bf16[272,640]{1,0:T(8,128)(2,1)S(1)}, bf16[272,640]{1,0:T(8,128)(2,1)S(1)}, u32[]{:S(2)}, u32[]{:S(2)}) collective-permute-start(bf16[272,640]{1,0:T(8,128)(2,1)S(1)} %pad_maximum_fusion.1.rest_16_), channel_id=1, source_target_pairs={{0,8},{4,12},{8,16},{12,20},{16,24},{20,28},{24,32},{28,36},{32,40... | collective-permute-start | bytes 1044488 | tf_op jit(solution)/shard_map/ppermute | solution.py:38
  4.0 4.0 %collective-permute-start.1 = (bf16[272,640]{1,0:T(8,128)(2,1)S(1)}, bf16[272,640]{1,0:T(8,128)(2,1)}, u32[]{:S(2)}, u32[]{:S(2)}) collective-permute-start(bf16[272,640]{1,0:T(8,128)(2,1)S(1)} %pad_maximum_fusion.1.rest_16_), channel_id=1, source_target_pairs={{0,56},{4,60},{8,0},{12,4},{16,8},{20,12},{24,16},{28,20},{32,24},... | collective-permute-start | bytes 1044488 | tf_op jit(solution)/shard_map/ppermute | solution.py:38
  8.0 0.1 convert_reduce_fusion
  8.1 0.1 convert_reduce_fusion.1
  8.2 0.1 pad_maximum_fusion.refs_0_.rest_0_.rest_8_
  8.3 0.6 collective-permute-start.9
  8.9 1.5 %collective-permute-start.7 = (bf16[528,640]{1,0:T(8,128)(2,1)S(1)}, bf16[528,640]{1,0:T(8,128)(2,1)S(1)}, u32[]{:S(2)}, u32[]{:S(2)}) collective-permute-start(bf16[528,640]{1,0:T(8,128)(2,1)S(1)} %pad_maximum_fusion.refs_0_.rest_0_.rest_8_), channel_id=1, source_target_pairs={{0,192},{4,196},{8,200},{12,204},{16,208},{20,212},{24,216},{28,22... | collective-permute-start | bytes 2027528 | tf_op jit(solution)/shard_map/ppermute | solution.py:38
  10.4 5.7 %collective-permute-done.rest_16_ = bf16[272,640]{1,0:T(8,128)(2,1)S(1)} collective-permute-done((bf16[272,640]{1,0:T(8,128)(2,1)S(1)}, bf16[272,640]{1,0:T(8,128)(2,1)S(1)}, u32[]{:S(2)}, u32[]{:S(2)}) %collective-permute-start) | collective-permute-done | bytes 348192 | tf_op jit(solution)/shard_map/ppermute | solution.py:38
  16.1 0.0 collective-permute-start.2
  16.1 3.2 %collective-permute-start.3 = (bf16[272,640]{1,0:T(8,128)(2,1)}, bf16[272,640]{1,0:T(8,128)(2,1)}, u32[]{:S(2)}, u32[]{:S(2)}) collective-permute-start(bf16[272,640]{1,0:T(8,128)(2,1)} %collective-permute-done.1.rest_17_), channel_id=1, source_target_pairs={{0,56},{4,60},{8,0},{12,4},{16,8},{20,12},{24,16},{28,20},{32,24},... | collective-permute-start | bytes 1044488 | tf_op jit(solution)/shard_map/ppermute | solution.py:38
  19.3 0.0 collective-permute-start.6
  19.3 7.4 %collective-permute-done.2.rest_16_ = bf16[272,640]{1,0:T(8,128)(2,1)} collective-permute-done((bf16[272,640]{1,0:T(8,128)(2,1)S(1)}, bf16[272,640]{1,0:T(8,128)(2,1)}, u32[]{:S(2)}, u32[]{:S(2)}) %collective-permute-start.2) | collective-permute-done | bytes 348192 | tf_op jit(solution)/shard_map/ppermute | solution.py:38
  26.8 0.0 collective-permute-start.4
  26.8 3.2 %collective-permute-start.5 = (bf16[272,640]{1,0:T(8,128)(2,1)}, bf16[272,640]{1,0:T(8,128)(2,1)S(1)}, u32[]{:S(2)}, u32[]{:S(2)}) collective-permute-start(bf16[272,640]{1,0:T(8,128)(2,1)} %collective-permute-done.3.rest_17_), channel_id=1, source_target_pairs={{0,56},{4,60},{8,0},{12,4},{16,8},{20,12},{24,16},{28,20},{32,24},... | collective-permute-start | bytes 1044488 | tf_op jit(solution)/shard_map/ppermute | solution.py:38
  30.0 0.1 pad_add_fusion.pos_ref
  30.1 0.6 collective-permute-start.10
  30.7 1.6 %collective-permute-start.13 = (bf16[256,640]{1,0:T(8,128)(2,1)S(1)}, bf16[256,640]{1,0:T(8,128)(2,1)S(1)}, u32[]{:S(2)}, u32[]{:S(2)}) collective-permute-start(bf16[256,640]{1,0:T(8,128)(2,1)S(1)} %slice.59), channel_id=1, source_target_pairs={{0,192},{4,196},{8,200},{12,204},{16,208},{20,212},{24,216},{28,22... | collective-permute-start | bytes 983048 | tf_op jit(solution)/shard_map/ppermute | solution.py:38
  32.3 4.2 %collective-permute-done.4.rest_16_ = bf16[272,640]{1,0:T(8,128)(2,1)S(1)} collective-permute-done((bf16[272,640]{1,0:T(8,128)(2,1)}, bf16[272,640]{1,0:T(8,128)(2,1)S(1)}, u32[]{:S(2)}, u32[]{:S(2)}) %collective-permute-start.4) | collective-permute-done | bytes 348192 | tf_op jit(solution)/shard_map/ppermute | solution.py:38
  36.6 0.0 collective-permute-start.8
  36.6 0.0 collective-permute-done.5.rest_17_
  36.6 0.5 collective-permute-start.12
  37.1 0.7 constant_dynamic-update-slice_fusion.4
  37.8 1.3 %collective-permute-done.13.rest_12_ = bf16[256,640]{1,0:T(8,128)(2,1)S(1)} collective-permute-done((bf16[256,640]{1,0:T(8,128)(2,1)S(1)}, bf16[256,640]{1,0:T(8,128)(2,1)S(1)}, u32[]{:S(2)}, u32[]{:S(2)}) %collective-permute-start.13) | collective-permute-done | bytes 327712 | tf_op jit(solution)/shard_map/ppermute | solution.py:38
  39.1 3.2 %collective-permute-start.16 = (bf16[144,640]{1,0:T(8,128)(2,1)S(1)}, bf16[144,640]{1,0:T(8,128)(2,1)S(1)}, u32[]{:S(2)}, u32[]{:S(2)}) collective-permute-start(bf16[144,640]{1,0:T(8,128)(2,1)S(1)} %slice.61), channel_id=1, source_target_pairs={{0,56},{4,60},{8,0},{12,4},{16,8},{20,12},{24,16},{28,20},{32,24},... | collective-permute-start | bytes 552968 | tf_op jit(solution)/shard_map/ppermute | solution.py:38
  42.4 0.7 constant_dynamic-update-slice_fusion.3
  43.1 2.8 %collective-permute-done.15.asked_ref.rest_16_ = bf16[144,640]{1,0:T(8,128)(2,1)S(1)} collective-permute-done((bf16[144,640]{1,0:T(8,128)(2,1)S(1)}, bf16[144,640]{1,0:T(8,128)(2,1)S(1)}, u32[]{:S(2)}, u32[]{:S(2)}) %collective-permute-start.15) | collective-permute-done | bytes 184352 | tf_op jit(solution)/shard_map/ppermute | solution.py:38
  45.9 0.0 collective-permute-done.16.rest_17_
  45.9 0.5 collective-permute-start.11
  46.4 0.7 constant_dynamic-update-slice_fusion.2
  47.1 2.2 %shard_map.61 = (f32[1,64,256]{2,1,0:T(8,128)S(1)}, s32[2,128]{1,0:T(2,128)S(1)}) custom-call(s32[3]{0:T(128)S(1)} %pad_add_fusion.pos_ref, bf16[144,640]{1,0:T(8,128)(2,1)S(1)} %collective-permute-done.15.asked_ref.rest_16_), custom_call_target="tpu_custom_call" | custom-call | flops 1000000 | bytes 1048576 | tf_op jit(solution)/shard_map/pallas_call | solution.py:102
  49.3 0.0 collective-permute-done.6.refs_1_.rest_1_.rest_9_
  49.3 0.0 collective-permute-done.12.refs_7_.rest_7_.rest_15_
  49.3 0.0 collective-permute-done.11.refs_5_.rest_5_
  49.3 2.3 %shard_map.62 = (bf16[672,128]{1,0:T(8,128)(2,1)S(1)}, bf16[672,128]{1,0:T(8,128)(2,1)S(1)}) custom-call(s32[2,128]{1,0:T(2,128)S(1)} %get-tuple-element.35.list_ref, bf16[64,640]{1,0:T(8,128)(2,1)S(1)} %get-tuple-element.28.mean_k_ref, bf16[64,640]{1,0:T(8,128)(2,1)S(1)} %get-tuple-element.29.mean_v_ref, f32[1,64,256]{2,1,0:T(8,128)S(1)} %get-tuple-element.36.bias_ref, ...), custom_call_target="tpu_custom_call" | custom-call | flops 1342177280 | bytes 4194304 | tf_op jit(solution)/shard_map/pallas_call | solution.py:306
  51.6 2.1 %collective-permute-start.17 = (bf16[672,128]{1,0:T(8,128)(2,1)S(1)}, bf16[672,128]{1,0:T(8,128)(2,1)S(1)}, u32[]{:S(2)}, u32[]{:S(2)}) collective-permute-start(bf16[672,128]{1,0:T(8,128)(2,1)S(1)} %get-tuple-element.38), channel_id=1, source_target_pairs={{0,56},{4,60},{8,0},{12,4},{16,8},{20,12},{24,16},{28,20},{32,24},... | collective-permute-start | bytes 516104 | tf_op jit(solution)/shard_map/ppermute | solution.py:38
  53.7 0.0 collective-permute-start.18
  53.8 4.2 %shard_map.55 = (f32[7,64,256]{2,1,0:T(8,128)S(1)}, s32[7,128]{1,0:T(8,128)S(1)}) custom-call(s32[3]{0:T(128)S(1)} %pad_add_fusion.pos_ref, bf16[112,128]{1,0:T(8,128)(2,1)S(1)} %constant_dynamic-update-slice_fusion.asked_ref), custom_call_target="tpu_custom_call" | custom-call | flops 1000000 | bytes 1048576 | tf_op jit(solution)/shard_map/pallas_call | solution.py:102
  58.0 1.9 %shard_map.60 = (bf16[672,256]{1,0:T(8,128)(2,1)S(1)}, bf16[672,256]{1,0:T(8,128)(2,1)S(1)}) custom-call(s32[7,128]{1,0:T(8,128)S(1)} %get-tuple-element.27.list_ref, bf16[64,640]{1,0:T(8,128)(2,1)S(1)} %get-tuple-element.28.mean_k_ref, bf16[64,640]{1,0:T(8,128)(2,1)S(1)} %get-tuple-element.29.mean_v_ref, f32[7,64,256]{2,1,0:T(8,128)S(1)} %get-tuple-element.30.bias_ref, ...), custom_call_target="tpu_custom_call" | custom-call | flops 1342177280 | bytes 4194304 | tf_op jit(solution)/shard_map/pallas_call | solution.py:306
  59.9 0.0 collective-permute-done.17.up_in_ref
  59.9 2.2 %collective-permute-done.18.down_in_ref = bf16[672,128]{1,0:T(8,128)(2,1)S(1)} collective-permute-done((bf16[672,128]{1,0:T(8,128)(2,1)S(1)}, bf16[672,128]{1,0:T(8,128)(2,1)S(1)}, u32[]{:S(2)}, u32[]{:S(2)}) %collective-permute-start.18) | collective-permute-done | bytes 172064 | tf_op jit(solution)/shard_map/ppermute | solution.py:38
  62.1 0.2 shard_map.63
  62.3 1.9 %collective-permute-start.19 = (bf16[672,256]{1,0:T(8,128)(2,1)S(1)}, bf16[672,256]{1,0:T(8,128)(2,1)S(1)}, u32[]{:S(2)}, u32[]{:S(2)}) collective-permute-start(bf16[672,256]{1,0:T(8,128)(2,1)S(1)} %get-tuple-element.41), channel_id=1, source_target_pairs={{0,56},{4,60},{8,0},{12,4},{16,8},{20,12},{24,16},{28,20},{32,24},... | collective-permute-start | bytes 1032200 | tf_op jit(solution)/shard_map/ppermute | solution.py:38
  64.3 0.2 collective-permute-start.20
  64.4 3.2 %shard_map.59 = (bf16[672,256]{1,0:T(8,128)(2,1)S(1)}, bf16[672,256]{1,0:T(8,128)(2,1)S(1)}) custom-call(s32[7,128]{1,0:T(8,128)S(1)} %get-tuple-element.27.list_ref, bf16[64,640]{1,0:T(8,128)(2,1)S(1)} %get-tuple-element.28.mean_k_ref, bf16[64,640]{1,0:T(8,128)(2,1)S(1)} %get-tuple-element.29.mean_v_ref, f32[7,64,256]{2,1,0:T(8,128)S(1)} %get-tuple-element.30.bias_ref, ...), custom_call_target="tpu_custom_call" | custom-call | flops 1342177280 | bytes 4194304 | tf_op jit(solution)/shard_map/pallas_call | solution.py:306
  67.7 4.8 %collective-permute-done.19.up_in_ref = bf16[672,256]{1,0:T(8,128)(2,1)S(1)} collective-permute-done((bf16[672,256]{1,0:T(8,128)(2,1)S(1)}, bf16[672,256]{1,0:T(8,128)(2,1)S(1)}, u32[]{:S(2)}, u32[]{:S(2)}) %collective-permute-start.19) | collective-permute-done | bytes 344096 | tf_op jit(solution)/shard_map/ppermute | solution.py:38
  72.5 3.4 %collective-permute-done.20.down_in_ref = bf16[672,256]{1,0:T(8,128)(2,1)S(1)} collective-permute-done((bf16[672,256]{1,0:T(8,128)(2,1)S(1)}, bf16[672,256]{1,0:T(8,128)(2,1)S(1)}, u32[]{:S(2)}, u32[]{:S(2)}) %collective-permute-start.20) | collective-permute-done | bytes 344096 | tf_op jit(solution)/shard_map/ppermute | solution.py:38
  75.9 0.3 shard_map.64
  76.2 0.3 collective-permute-start.21
  76.5 1.8 %collective-permute-start.22 = (bf16[672,256]{1,0:T(8,128)(2,1)S(1)}, bf16[672,256]{1,0:T(8,128)(2,1)S(1)}, u32[]{:S(2)}, u32[]{:S(2)}) collective-permute-start(bf16[672,256]{1,0:T(8,128)(2,1)S(1)} %get-tuple-element.46), channel_id=1, source_target_pairs={{0,8},{4,12},{8,16},{12,20},{16,24},{20,28},{24,32},{28,36},{32,40... | collective-permute-start | bytes 1032200 | tf_op jit(solution)/shard_map/ppermute | solution.py:38
  78.3 3.3 %shard_map.58 = (bf16[672,256]{1,0:T(8,128)(2,1)S(1)}, bf16[672,256]{1,0:T(8,128)(2,1)S(1)}) custom-call(s32[7,128]{1,0:T(8,128)S(1)} %get-tuple-element.27.list_ref, bf16[64,640]{1,0:T(8,128)(2,1)S(1)} %get-tuple-element.28.mean_k_ref, bf16[64,640]{1,0:T(8,128)(2,1)S(1)} %get-tuple-element.29.mean_v_ref, f32[7,64,256]{2,1,0:T(8,128)S(1)} %get-tuple-element.30.bias_ref, ...), custom_call_target="tpu_custom_call" | custom-call | flops 1342177280 | bytes 4194304 | tf_op jit(solution)/shard_map/pallas_call | solution.py:306
  81.6 4.3 %collective-permute-done.21.up_in_ref = bf16[672,256]{1,0:T(8,128)(2,1)S(1)} collective-permute-done((bf16[672,256]{1,0:T(8,128)(2,1)S(1)}, bf16[672,256]{1,0:T(8,128)(2,1)S(1)}, u32[]{:S(2)}, u32[]{:S(2)}) %collective-permute-start.21) | collective-permute-done | bytes 344096 | tf_op jit(solution)/shard_map/ppermute | solution.py:38
  85.8 1.4 %collective-permute-done.22.down_in_ref = bf16[672,256]{1,0:T(8,128)(2,1)S(1)} collective-permute-done((bf16[672,256]{1,0:T(8,128)(2,1)S(1)}, bf16[672,256]{1,0:T(8,128)(2,1)S(1)}, u32[]{:S(2)}, u32[]{:S(2)}) %collective-permute-start.22) | collective-permute-done | bytes 344096 | tf_op jit(solution)/shard_map/ppermute | solution.py:38
  87.2 0.3 shard_map.65
  87.5 0.4 collective-permute-start.23
  87.9 1.7 %collective-permute-start.24 = (bf16[672,256]{1,0:T(8,128)(2,1)S(1)}, bf16[672,256]{1,0:T(8,128)(2,1)S(1)}, u32[]{:S(2)}, u32[]{:S(2)}) collective-permute-start(bf16[672,256]{1,0:T(8,128)(2,1)S(1)} %get-tuple-element.48), channel_id=1, source_target_pairs={{0,8},{4,12},{8,16},{12,20},{16,24},{20,28},{24,32},{28,36},{32,40... | collective-permute-start | bytes 1032200 | tf_op jit(solution)/shard_map/ppermute | solution.py:38
  89.6 1.3 %shard_map.57.own_ref = bf16[672,256]{1,0:T(8,128)(2,1)S(1)} custom-call(s32[7,128]{1,0:T(8,128)S(1)} %get-tuple-element.27.list_ref, bf16[64,640]{1,0:T(8,128)(2,1)S(1)} %get-tuple-element.28.mean_k_ref, bf16[64,640]{1,0:T(8,128)(2,1)S(1)} %get-tuple-element.29.mean_v_ref, f32[7,64,256]{2,1,0:T(8,128)S(1)} %get-tuple-element.30.bias_ref, ...), custom_call_target="tpu_custom_call" | custom-call | flops 1342177280 | bytes 4194304 | tf_op jit(solution)/shard_map/pallas_call | solution.py:306
  91.0 5.2 %collective-permute-done.23.up_ref = bf16[672,256]{1,0:T(8,128)(2,1)S(1)} collective-permute-done((bf16[672,256]{1,0:T(8,128)(2,1)S(1)}, bf16[672,256]{1,0:T(8,128)(2,1)S(1)}, u32[]{:S(2)}, u32[]{:S(2)}) %collective-permute-start.23) | collective-permute-done | bytes 344096 | tf_op jit(solution)/shard_map/ppermute | solution.py:38
  96.2 1.5 %collective-permute-done.24.down_ref = bf16[672,256]{1,0:T(8,128)(2,1)S(1)} collective-permute-done((bf16[672,256]{1,0:T(8,128)(2,1)S(1)}, bf16[672,256]{1,0:T(8,128)(2,1)S(1)}, u32[]{:S(2)}, u32[]{:S(2)}) %collective-permute-start.24) | collective-permute-done | bytes 344096 | tf_op jit(solution)/shard_map/ppermute | solution.py:38
  97.7 1.0 %shard_map.66 = bf16[256,640]{1,0:T(8,128)(2,1)} custom-call(bf16[672,256]{1,0:T(8,128)(2,1)S(1)} %shard_map.57.own_ref, bf16[672,256]{1,0:T(8,128)(2,1)S(1)} %collective-permute-done.23.up_ref, bf16[672,256]{1,0:T(8,128)(2,1)S(1)} %collective-permute-done.24.down_ref), custom_call_target="tpu_custom_call" | custom-call | tf_op jit(solution)/shard_map/pallas_call | solution.py:381
  (24 shorter events, 0.2 us)
Async XLA Ops:
  0.9 7.2 %copy-start = (bf16[256,640]{1,0:T(8,128)(2,1)S(1)}, bf16[256,640]{1,0:T(8,128)(2,1)}, u32[]{:S(2)}) copy-start(bf16[256,640]{1,0:T(8,128)(2,1)} %param.7) | copy-start | bytes 983044
  2.0 6.2 %copy-start.1 = (bf16[256,640]{1,0:T(8,128)(2,1)S(1)}, bf16[256,640]{1,0:T(8,128)(2,1)}, u32[]{:S(2)}) copy-start(bf16[256,640]{1,0:T(8,128)(2,1)} %param.6) | copy-start | bytes 983044
  2.0 14.1 %collective-permute-start = (bf16[272,640]{1,0:T(8,128)(2,1)S(1)}, bf16[272,640]{1,0:T(8,128)(2,1)S(1)}, u32[]{:S(2)}, u32[]{:S(2)}) collective-permute-start(bf16[272,640]{1,0:T(8,128)(2,1)S(1)} %pad_maximum_fusion.1.rest_16_), channel_id=1, source_target_pairs={{0,8},{4,12},{8,16},{12,20},{16,24},{20,28},{24,32},{28,36},{32,40... | collective-permute-start | bytes 1044488 | tf_op jit(solution)/shard_map/ppermute | solution.py:38
  4.0 12.1 %collective-permute-start.1 = (bf16[272,640]{1,0:T(8,128)(2,1)S(1)}, bf16[272,640]{1,0:T(8,128)(2,1)}, u32[]{:S(2)}, u32[]{:S(2)}) collective-permute-start(bf16[272,640]{1,0:T(8,128)(2,1)S(1)} %pad_maximum_fusion.1.rest_16_), channel_id=1, source_target_pairs={{0,56},{4,60},{8,0},{12,4},{16,8},{20,12},{24,16},{28,20},{32,24},... | collective-permute-start | bytes 1044488 | tf_op jit(solution)/shard_map/ppermute | solution.py:38
  8.3 21.8 %collective-permute-start.9 = (bf16[528,640]{1,0:T(8,128)(2,1)S(1)}, bf16[528,640]{1,0:T(8,128)(2,1)S(1)}, u32[]{:S(2)}, u32[]{:S(2)}) collective-permute-start(bf16[528,640]{1,0:T(8,128)(2,1)S(1)} %pad_maximum_fusion.refs_0_.rest_0_.rest_8_), channel_id=1, source_target_pairs={{0,64},{4,68},{8,72},{12,76},{16,80},{20,84},{24,88},{28,92},{32,9... | collective-permute-start | bytes 2027528 | tf_op jit(solution)/shard_map/ppermute | solution.py:38
  8.9 21.8 %collective-permute-start.7 = (bf16[528,640]{1,0:T(8,128)(2,1)S(1)}, bf16[528,640]{1,0:T(8,128)(2,1)S(1)}, u32[]{:S(2)}, u32[]{:S(2)}) collective-permute-start(bf16[528,640]{1,0:T(8,128)(2,1)S(1)} %pad_maximum_fusion.refs_0_.rest_0_.rest_8_), channel_id=1, source_target_pairs={{0,192},{4,196},{8,200},{12,204},{16,208},{20,212},{24,216},{28,22... | collective-permute-start | bytes 2027528 | tf_op jit(solution)/shard_map/ppermute | solution.py:38
  16.1 10.7 %collective-permute-start.2 = (bf16[272,640]{1,0:T(8,128)(2,1)S(1)}, bf16[272,640]{1,0:T(8,128)(2,1)}, u32[]{:S(2)}, u32[]{:S(2)}) collective-permute-start(bf16[272,640]{1,0:T(8,128)(2,1)S(1)} %collective-permute-done.rest_16_), channel_id=1, source_target_pairs={{0,8},{4,12},{8,16},{12,20},{16,24},{20,28},{24,32},{28,36},{32,40... | collective-permute-start | bytes 1044488 | tf_op jit(solution)/shard_map/ppermute | solution.py:38
  16.1 10.7 %collective-permute-start.3 = (bf16[272,640]{1,0:T(8,128)(2,1)}, bf16[272,640]{1,0:T(8,128)(2,1)}, u32[]{:S(2)}, u32[]{:S(2)}) collective-permute-start(bf16[272,640]{1,0:T(8,128)(2,1)} %collective-permute-done.1.rest_17_), channel_id=1, source_target_pairs={{0,56},{4,60},{8,0},{12,4},{16,8},{20,12},{24,16},{28,20},{32,24},... | collective-permute-start | bytes 1044488 | tf_op jit(solution)/shard_map/ppermute | solution.py:38
  19.3 29.9 %collective-permute-start.6 = (bf16[528,640]{1,0:T(8,128)(2,1)S(1)}, bf16[528,640]{1,0:T(8,128)(2,1)S(1)}, u32[]{:S(2)}, u32[]{:S(2)}) collective-permute-start(bf16[528,640]{1,0:T(8,128)(2,1)S(1)} %pad_maximum_fusion.refs_0_.rest_0_.rest_8_), channel_id=1, source_target_pairs={{0,4},{4,0},{8,12},{12,8},{16,20},{20,16},{24,28},{28,24},{32,36},... | collective-permute-start | bytes 2027528 | tf_op jit(solution)/shard_map/ppermute | solution.py:38
  26.8 9.8 %collective-permute-start.4 = (bf16[272,640]{1,0:T(8,128)(2,1)}, bf16[272,640]{1,0:T(8,128)(2,1)S(1)}, u32[]{:S(2)}, u32[]{:S(2)}) collective-permute-start(bf16[272,640]{1,0:T(8,128)(2,1)} %collective-permute-done.2.rest_16_), channel_id=1, source_target_pairs={{0,8},{4,12},{8,16},{12,20},{16,24},{20,28},{24,32},{28,36},{32,40... | collective-permute-start | bytes 1044488 | tf_op jit(solution)/shard_map/ppermute | solution.py:38
  26.8 9.8 %collective-permute-start.5 = (bf16[272,640]{1,0:T(8,128)(2,1)}, bf16[272,640]{1,0:T(8,128)(2,1)S(1)}, u32[]{:S(2)}, u32[]{:S(2)}) collective-permute-start(bf16[272,640]{1,0:T(8,128)(2,1)} %collective-permute-done.3.rest_17_), channel_id=1, source_target_pairs={{0,56},{4,60},{8,0},{12,4},{16,8},{20,12},{24,16},{28,20},{32,24},... | collective-permute-start | bytes 1044488 | tf_op jit(solution)/shard_map/ppermute | solution.py:38
  30.1 9.0 %collective-permute-start.10 = (bf16[272,640]{1,0:T(8,128)(2,1)S(1)}, bf16[272,640]{1,0:T(8,128)(2,1)S(1)}, u32[]{:S(2)}, u32[]{:S(2)}) collective-permute-start(bf16[272,640]{1,0:T(8,128)(2,1)S(1)} %slice.58), channel_id=1, source_target_pairs={{0,64},{4,68},{8,72},{12,76},{16,80},{20,84},{24,88},{28,92},{32,9... | collective-permute-start | bytes 1044488 | tf_op jit(solution)/shard_map/ppermute | solution.py:38
  30.7 8.4 %collective-permute-start.13 = (bf16[256,640]{1,0:T(8,128)(2,1)S(1)}, bf16[256,640]{1,0:T(8,128)(2,1)S(1)}, u32[]{:S(2)}, u32[]{:S(2)}) collective-permute-start(bf16[256,640]{1,0:T(8,128)(2,1)S(1)} %slice.59), channel_id=1, source_target_pairs={{0,192},{4,196},{8,200},{12,204},{16,208},{20,212},{24,216},{28,22... | collective-permute-start | bytes 983048 | tf_op jit(solution)/shard_map/ppermute | solution.py:38
  36.6 12.7 %collective-permute-start.8 = (bf16[528,640]{1,0:T(8,128)(2,1)S(1)}, bf16[528,640]{1,0:T(8,128)(2,1)S(1)}, u32[]{:S(2)}, u32[]{:S(2)}) collective-permute-start(bf16[528,640]{1,0:T(8,128)(2,1)S(1)} %collective-permute-done.7.refs_2_.rest_2_.rest_10_), channel_id=1, source_target_pairs={{0,4},{4,0},{8,12},{12,8},{16,20},{20,16},{24,28},{28,24},{32,36},... | collective-permute-start | bytes 2027528 | tf_op jit(solution)/shard_map/ppermute | solution.py:38
  36.6 12.7 %collective-permute-start.12 = (bf16[528,640]{1,0:T(8,128)(2,1)S(1)}, bf16[528,640]{1,0:T(8,128)(2,1)S(1)}, u32[]{:S(2)}, u32[]{:S(2)}) collective-permute-start(bf16[528,640]{1,0:T(8,128)(2,1)S(1)} %collective-permute-done.9.refs_6_.rest_6_.rest_14_), channel_id=1, source_target_pairs={{0,4},{4,0},{8,12},{12,8},{16,20},{20,16},{24,28},{28,24},{32,36},... | collective-permute-start | bytes 2027528 | tf_op jit(solution)/shard_map/ppermute | solution.py:38
  39.1 6.7 %collective-permute-start.15 = (bf16[144,640]{1,0:T(8,128)(2,1)S(1)}, bf16[144,640]{1,0:T(8,128)(2,1)S(1)}, u32[]{:S(2)}, u32[]{:S(2)}) collective-permute-start(bf16[144,640]{1,0:T(8,128)(2,1)S(1)} %slice.60), channel_id=1, source_target_pairs={{0,8},{4,12},{8,16},{12,20},{16,24},{20,28},{24,32},{28,36},{32,40... | collective-permute-start | bytes 552968 | tf_op jit(solution)/shard_map/ppermute | solution.py:38
  39.1 6.7 %collective-permute-start.16 = (bf16[144,640]{1,0:T(8,128)(2,1)S(1)}, bf16[144,640]{1,0:T(8,128)(2,1)S(1)}, u32[]{:S(2)}, u32[]{:S(2)}) collective-permute-start(bf16[144,640]{1,0:T(8,128)(2,1)S(1)} %slice.61), channel_id=1, source_target_pairs={{0,56},{4,60},{8,0},{12,4},{16,8},{20,12},{24,16},{28,20},{32,24},... | collective-permute-start | bytes 552968 | tf_op jit(solution)/shard_map/ppermute | solution.py:38
  45.9 3.4 %collective-permute-start.14 = (bf16[256,640]{1,0:T(8,128)(2,1)S(1)}, bf16[256,640]{1,0:T(8,128)(2,1)S(1)}, u32[]{:S(2)}, u32[]{:S(2)}) collective-permute-start(bf16[256,640]{1,0:T(8,128)(2,1)S(1)} %collective-permute-done.13.rest_12_), channel_id=1, source_target_pairs={{0,4},{4,0},{8,12},{12,8},{16,20},{20,16},{24,28},{28,24},{32,36},... | collective-permute-start | bytes 983048 | tf_op jit(solution)/shard_map/ppermute | solution.py:38
  45.9 3.4 %collective-permute-start.11 = (bf16[272,640]{1,0:T(8,128)(2,1)S(1)}, bf16[272,640]{1,0:T(8,128)(2,1)S(1)}, u32[]{:S(2)}, u32[]{:S(2)}) collective-permute-start(bf16[272,640]{1,0:T(8,128)(2,1)S(1)} %collective-permute-done.10.refs_4_.rest_4_), channel_id=1, source_target_pairs={{0,4},{4,0},{8,12},{12,8},{16,20},{20,16},{24,28},{28,24},{32,36},... | collective-permute-start | bytes 1044488 | tf_op jit(solution)/shard_map/ppermute | solution.py:38
  51.6 8.3 %collective-permute-start.17 = (bf16[672,128]{1,0:T(8,128)(2,1)S(1)}, bf16[672,128]{1,0:T(8,128)(2,1)S(1)}, u32[]{:S(2)}, u32[]{:S(2)}) collective-permute-start(bf16[672,128]{1,0:T(8,128)(2,1)S(1)} %get-tuple-element.38), channel_id=1, source_target_pairs={{0,56},{4,60},{8,0},{12,4},{16,8},{20,12},{24,16},{28,20},{32,24},... | collective-permute-start | bytes 516104 | tf_op jit(solution)/shard_map/ppermute | solution.py:38
  53.7 8.4 %collective-permute-start.18 = (bf16[672,128]{1,0:T(8,128)(2,1)S(1)}, bf16[672,128]{1,0:T(8,128)(2,1)S(1)}, u32[]{:S(2)}, u32[]{:S(2)}) collective-permute-start(bf16[672,128]{1,0:T(8,128)(2,1)S(1)} %get-tuple-element.40), channel_id=1, source_target_pairs={{0,8},{4,12},{8,16},{12,20},{16,24},{20,28},{24,32},{28,36},{32,40... | collective-permute-start | bytes 516104 | tf_op jit(solution)/shard_map/ppermute | solution.py:38
  62.3 10.1 %collective-permute-start.19 = (bf16[672,256]{1,0:T(8,128)(2,1)S(1)}, bf16[672,256]{1,0:T(8,128)(2,1)S(1)}, u32[]{:S(2)}, u32[]{:S(2)}) collective-permute-start(bf16[672,256]{1,0:T(8,128)(2,1)S(1)} %get-tuple-element.41), channel_id=1, source_target_pairs={{0,56},{4,60},{8,0},{12,4},{16,8},{20,12},{24,16},{28,20},{32,24},... | collective-permute-start | bytes 1032200 | tf_op jit(solution)/shard_map/ppermute | solution.py:38
  64.3 11.6 %collective-permute-start.20 = (bf16[672,256]{1,0:T(8,128)(2,1)S(1)}, bf16[672,256]{1,0:T(8,128)(2,1)S(1)}, u32[]{:S(2)}, u32[]{:S(2)}) collective-permute-start(bf16[672,256]{1,0:T(8,128)(2,1)S(1)} %get-tuple-element.43), channel_id=1, source_target_pairs={{0,8},{4,12},{8,16},{12,20},{16,24},{20,28},{24,32},{28,36},{32,40... | collective-permute-start | bytes 1032200 | tf_op jit(solution)/shard_map/ppermute | solution.py:38
  76.2 9.7 %collective-permute-start.21 = (bf16[672,256]{1,0:T(8,128)(2,1)S(1)}, bf16[672,256]{1,0:T(8,128)(2,1)S(1)}, u32[]{:S(2)}, u32[]{:S(2)}) collective-permute-start(bf16[672,256]{1,0:T(8,128)(2,1)S(1)} %get-tuple-element.44), channel_id=1, source_target_pairs={{0,56},{4,60},{8,0},{12,4},{16,8},{20,12},{24,16},{28,20},{32,24},... | collective-permute-start | bytes 1032200 | tf_op jit(solution)/shard_map/ppermute | solution.py:38
  76.5 10.7 %collective-permute-start.22 = (bf16[672,256]{1,0:T(8,128)(2,1)S(1)}, bf16[672,256]{1,0:T(8,128)(2,1)S(1)}, u32[]{:S(2)}, u32[]{:S(2)}) collective-permute-start(bf16[672,256]{1,0:T(8,128)(2,1)S(1)} %get-tuple-element.46), channel_id=1, source_target_pairs={{0,8},{4,12},{8,16},{12,20},{16,24},{20,28},{24,32},{28,36},{32,40... | collective-permute-start | bytes 1032200 | tf_op jit(solution)/shard_map/ppermute | solution.py:38
  87.5 8.7 %collective-permute-start.23 = (bf16[672,256]{1,0:T(8,128)(2,1)S(1)}, bf16[672,256]{1,0:T(8,128)(2,1)S(1)}, u32[]{:S(2)}, u32[]{:S(2)}) collective-permute-start(bf16[672,256]{1,0:T(8,128)(2,1)S(1)} %get-tuple-element.47), channel_id=1, source_target_pairs={{0,56},{4,60},{8,0},{12,4},{16,8},{20,12},{24,16},{28,20},{32,24},... | collective-permute-start | bytes 1032200 | tf_op jit(solution)/shard_map/ppermute | solution.py:38
  87.9 9.9 %collective-permute-start.24 = (bf16[672,256]{1,0:T(8,128)(2,1)S(1)}, bf16[672,256]{1,0:T(8,128)(2,1)S(1)}, u32[]{:S(2)}, u32[]{:S(2)}) collective-permute-start(bf16[672,256]{1,0:T(8,128)(2,1)S(1)} %get-tuple-element.48), channel_id=1, source_target_pairs={{0,8},{4,12},{8,16},{12,20},{16,24},{20,28},{24,32},{28,36},{32,40... | collective-permute-start | bytes 1032200 | tf_op jit(solution)/shard_map/ppermute | solution.py:38
where the time goes:
time: 98.5 us; the launch traced here: 98.7 us
  waiting for transfers between devices  44.3 us (45%)
  starting transfers between devices  29.5 us (30%)
  Pallas kernels  20.2 us (21%)
  local copies, waits for them, and re-layouts  3.37 us (3%)
  other arithmetic  1.1 us (1%)
    ppermute x25, waiting for transfers between devices, move(): return lax.ppermute(array, 'ctx', pairs)  44.3 us
    ppermute x25, starting transfers between devices, move(): return lax.ppermute(array, 'ctx', pairs)  29.5 us
    pallas_call x5, Pallas kernels, part(): pl.pallas_call(functools.partial(part_kernel, heads, groups), in_specs=[s...  12 us
    pallas_call x2, Pallas kernels, make_lists(): pl.pallas_call(functools.partial(list_kernel, first, spec), in_specs=[sme...  6.39 us
    unnamed x10, local copies, waits for them, and re-layouts  2.09 us
  transfers between devices with their start and end apart: 25, of which 12 were waited for; matrix products, arithmetic and copies ran while one was open for 3% of the time, Pallas kernels for 16%

commit v1 on v0

--- a/solution.py
+++ b/solution.py
@@ -62,22 +62,15 @@
     ids_copy.wait()
 
     for g, (table, low, high) in enumerate(spec):
-
-        def ask(b, n, g=g, table=table):
+        for n in range(FIRST + MOST):
+            list_ref[g, ENTRY + n] = -1
+        used = jnp.int32(0)
+        for b in range(low, high):
             for p in range(SLOTS):
                 code = ids_ref[table, b, p]
-                list_ref[g, ENTRY + n] = code
-                n = n + (code >= 0).astype(jnp.int32)
-            return n
-
-        used = lax.fori_loop(low, high, ask, jnp.int32(0))
+                list_ref[g, ENTRY + used] = code
+                used = used + (code >= 0).astype(jnp.int32)
         list_ref[g, 0] = used
-
-        def blank(n, carry, g=g):
-            list_ref[g, ENTRY + n] = -1
-            return carry
-
-        lax.fori_loop(used, FIRST + MOST, blank, 0)
 
     shape = (MEAN_KEYS, TOKENS)
     key_ids, token_blocks = iota(shape, 0), iota(shape, 1) // BLOCK
@@ -168,7 +161,11 @@
     key_refs, rest = rest[:PLANE], rest[PLANE:]
     value_refs, rest = rest[:PLANE], rest[PLANE:]
     q_refs, rest = rest[:count], rest[count:]
-    out_refs, rest = rest[:count], rest[count:]
+    out_refs = []
+    for group in groups:
+        halves = group[2] * BLOCK // HALF
+        out_refs.append(rest[:halves])
+        rest = rest[halves:]
     accs, rest = rest[:count], rest[count:]
     tops, rest = rest[:count], rest[count:]
     sums, bufs = rest[:count], rest[count:]
@@ -279,17 +276,20 @@
         top = tops[g][...]
         sent = top.astype(jnp.bfloat16).astype(jnp.float32)
         factor = jnp.exp(top - sent)
-        for h, cols in enumerate(all_cols):
-            out_refs[g][cols] = (accs[g][cols] * factor[h : h + 1]).astype(jnp.bfloat16)
-        write_stats(out_refs[g], slice(None), heads, sent, sums[g][...] * factor)
-
-
-def write_stats(out_ref, lanes, heads, top, total):
+        total = sums[g][...] * factor
+        for half, out_ref in enumerate(out_refs[g]):
+            lanes = slice(half * HALF, (half + 1) * HALF)
+            for h, cols in enumerate(all_cols):
+                out_ref[cols] = (accs[g][cols, lanes] * factor[h : h + 1, lanes]).astype(jnp.bfloat16)
+            write_stats(out_ref, heads, sent[:, lanes], total[:, lanes])
+
+
+def write_stats(out_ref, heads, top, total):
     high = total.astype(jnp.bfloat16).astype(jnp.float32)
     rows = (top, high, total - high, jnp.zeros_like(top))
     valid = iota(top.shape, 0) < heads
     rows = [jnp.where(valid, r, 0.0) for r in rows]
-    out_ref[heads * HD :, lanes] = jnp.concatenate(rows, axis=0).astype(jnp.bfloat16)
+    out_ref[heads * HD :] = jnp.concatenate(rows, axis=0).astype(jnp.bfloat16)
 
 
 def part(plane, bias, lists, queries, groups):
@@ -306,8 +306,9 @@
     return pl.pallas_call(
         functools.partial(part_kernel, heads, groups),
         in_specs=[smem] + [vmem] * len(operands),
-        out_specs=[vmem] * len(groups),
-        out_shape=[jax.ShapeDtypeStruct((columns + STATS, w), jnp.bfloat16) for w in widths],
+        out_specs=[vmem] * (sum(widths) // HALF),
+        out_shape=[jax.ShapeDtypeStruct((columns + STATS, HALF), jnp.bfloat16)]
+        * (sum(widths) // HALF),
         scratch_shapes=scratch,
         compiler_params=PARAMS,
         cost_estimate=pl.CostEstimate(
@@ -316,73 +317,61 @@
     )(lists, *operands)
 
 
-def stats_of(ref, lanes, heads):
-    rows = ref[heads * HD :, lanes].astype(jnp.float32)
-    return rows[:8], rows[8:16] + rows[16:24]
-
-
-def merged(heads, parts):
-    stats = [stats_of(ref, lanes, heads) for ref, lanes in parts]
-    top = functools.reduce(jnp.maximum, [s[0] for s in stats])
-    ratios = [jnp.exp(s[0] - top) for s in stats]
-    total = functools.reduce(jnp.add, [r * s[1] for r, s in zip(ratios, stats)])
-    return top, ratios, total
-
-
-def merge_kernel(heads, up_ref, up_in_ref, down_ref, down_in_ref, up_out, down_out):
-    for own, came, out, up in (
-        (up_ref, up_in_ref, up_out, True),
-        (down_ref, down_in_ref, down_out, False),
-    ):
-        width = came.shape[1]
-        if width == own.shape[1]:
-            lanes = slice(None)
-        else:
-            lanes = slice(0, width) if up else slice(width, 2 * width)
-            rest = slice(width, 2 * width) if up else slice(0, width)
-            out[:, rest] = own[:, rest]
-        top, ratios, total = merged(heads, ((own, lanes), (came, slice(None))))
+def merged(heads, refs):
+    stats = [ref[heads * HD :].astype(jnp.float32) for ref in refs]
+    top = functools.reduce(jnp.maximum, [s[:8] for s in stats])
+    ratios = [jnp.exp(s[:8] - top) for s in stats]
+    totals = [r * (s[8:16] + s[16:24]) for r, s in zip(ratios, stats)]
+    return top, ratios, functools.reduce(jnp.add, totals)
+
+
+def merge_kernel(heads, *refs):
+    count = len(refs) // 3
+    for own, came, out in zip(refs[:count], refs[count : 2 * count], refs[2 * count :]):
+        top, ratios, total = merged(heads, (own, came))
         for h in range(heads):
             cols = pl.ds(h * HD, HD)
-            one = own[cols, lanes].astype(jnp.float32) * ratios[0][h : h + 1]
-            two = came[cols, :].astype(jnp.float32) * ratios[1][h : h + 1]
-            out[cols, lanes] = (one + two).astype(jnp.bfloat16)
-        write_stats(out, lanes, heads, top, total)
-
-
-def merge(up, up_in, down, down_in):
-    heads = (up.shape[0] - STATS) // HD
-    whole = jax.ShapeDtypeStruct(up.shape, jnp.bfloat16)
+            one = own[cols].astype(jnp.float32) * ratios[0][h : h + 1]
+            two = came[cols].astype(jnp.float32) * ratios[1][h : h + 1]
+            out[cols] = (one + two).astype(jnp.bfloat16)
+        write_stats(out, heads, top, total)
+
+
+def merge(owns, cames):
+    heads = (owns[0].shape[0] - STATS) // HD
     return pl.pallas_call(
         functools.partial(merge_kernel, heads),
-        out_shape=(whole, whole),
+        out_shape=[jax.ShapeDtypeStruct(own.shape, jnp.bfloat16) for own in owns],
         compiler_params=PARAMS,
         cost_estimate=pl.CostEstimate(
-            flops=1000000, bytes_accessed=2 * 1024 * 1024, transcendentals=1000
+            flops=1000000, bytes_accessed=1024 * 1024, transcendentals=1000
         ),
-    )(up, up_in, down, down_in)
-
-
-def last_kernel(heads, own_ref, up_ref, down_ref, out_ref):
-    refs = (own_ref, up_ref, down_ref)
-    _, ratios, total = merged(heads, [(ref, slice(None)) for ref in refs])
-    valid = iota(total.shape, 0) < heads
-    scales = [r / jnp.where(valid, total, 1.0) for r in ratios]
-    for h in range(heads):
-        cols = pl.ds(h * HD, HD)
-        whole = jnp.zeros((HD, TOKENS), jnp.float32)
-        for ref, scale in zip(refs, scales):
-            whole = whole + ref[cols].astype(jnp.float32) * scale[h : h + 1]
-        out_ref[:, cols] = jnp.transpose(whole).astype(out_ref.dtype)
-
-
-def last(own, up, down):
-    columns = own.shape[0] - STATS
+    )(*owns, *cames)
+
+
+def last_kernel(heads, *refs):
+    out_ref = refs[-1]
+    for half in range(2):
+        parts = refs[half : len(refs) - 1 : 2]
+        _, ratios, total = merged(heads, parts)
+        valid = iota(total.shape, 0) < heads
+        scales = [r / jnp.where(valid, total, 1.0) for r in ratios]
+        rows = pl.ds(half * HALF, HALF)
+        for h in range(heads):
+            cols = pl.ds(h * HD, HD)
+            whole = jnp.zeros((HD, HALF), jnp.float32)
+            for ref, scale in zip(parts, scales):
+                whole = whole + ref[cols].astype(jnp.float32) * scale[h : h + 1]
+            out_ref[rows, cols] = jnp.transpose(whole).astype(out_ref.dtype)
+
+
+def last(parts):
+    columns = parts[0].shape[0] - STATS
     return pl.pallas_call(
         functools.partial(last_kernel, columns // HD),
         out_shape=jax.ShapeDtypeStruct((TOKENS, columns), jnp.bfloat16),
         compiler_params=PARAMS,
-    )(own, up, down)
+    )(*parts)
 
 
 def body(queries, key_tokens, value_tokens, pair_keys, pair_count):
@@ -415,13 +404,8 @@
     far_k, far_v = move(left[:split], dx=1), move(right[split:], dx=-1)
     left_twin, right_twin = move(left, dc=1), move(right, dc=1)
     up3, down3 = move(up2, dz=1), move(down2, dz=-1)
-    far_k_twin, far_v_twin = move(far_k, dc=1), move(far_v, dc=1)
     far_up = move(up3[: HALF + REQUEST], dz=1)
     far_down = move(down3[HALF:], dz=-1)
-    far_up, far_down = barrier((far_up, far_down))
-    key_refs = (own, own_twin, right, right_twin, far_k, far_k_twin, left, left_twin)
-    value_refs = (own, own_twin, right, right_twin, far_v, far_v_twin, left, left_twin)
-    plane = (*gather_means(key_refs), key_refs, value_refs)
     payloads = (pay, up1, down1, up2, down2, up3, down3)
     requests = [p[HALF : HALF + REQUEST, :HD] for p in payloads]
     tables = len(payloads)
@@ -432,21 +416,33 @@
         tables,
         tuple((table, 0, BLOCKS) for table in range(tables)),
     )
+    far_k, far_v, *near = barrier((far_k, far_v, *near))
+    far_k_twin, far_v_twin = move(far_k, dc=1), move(far_v, dc=1)
+    key_refs = (own, own_twin, right, right_twin, far_k, far_k_twin, left, left_twin)
+    value_refs = (own, own_twin, right, right_twin, far_v, far_v_twin, left, left_twin)
+    plane = (*gather_means(key_refs), key_refs, value_refs)
+    far_up, far_down = barrier((far_up, far_down))
     both, mid = (0, HALF + REQUEST), BLOCKS // 2
     far = make_lists(position, far_up, HALF, 1, ((0, 0, mid), (0, mid, BLOCKS)))
 
-    up_in, down_in = part(
+    up_a, down_b = part(
         plane, *far, (far_up, far_down), (((0,), 0, mid, 0, 0), ((REQUEST,), mid, mid, 1, 0))
     )
-    up_in, down_in = move(up_in, dz=-1), move(down_in, dz=1)
+    up_a, down_b = move(up_a, dz=-1), move(down_b, dz=1)
+    up_b = down_a = None
     for hop, up, down in ((3, up3, down3), (2, up2, down2), (1, up1, down1)):
         first = 2 * hop - 1
         groups = tuple((both, 0, BLOCKS, first + i, first + i) for i in range(2))
-        up_part, down_part = part(plane, *near, (up, down), groups)
-        up_sum, down_sum = merge(up_part, up_in, down_part, down_in)
-        up_in, down_in = move(up_sum, dz=-1), move(down_sum, dz=1)
-    (own_part,) = part(plane, *near, (pay,), ((both, 0, BLOCKS, 0, 0),))
-    return last(own_part, up_in, down_in)
+        own_up_a, own_up_b, own_down_a, own_down_b = part(plane, *near, (up, down), groups)
+        if up_b is None:
+            up_b, down_a = own_up_b, own_down_a
+        else:
+            up_b, down_a = merge((own_up_b, own_down_a), (up_b, down_a))
+        up_b, down_a = move(up_b, dz=-1), move(down_a, dz=1)
+        up_a, down_b = merge((own_up_a, own_down_b), (up_a, down_b))
+        up_a, down_b = move(up_a, dz=-1), move(down_b, dz=1)
+    own_a, own_b = part(plane, *near, (pay,), ((both, 0, BLOCKS, 0, 0),))
+    return last((own_a, own_b, up_a, up_b, down_a, down_b))
 
 
 def solution(mesh):

time: 98.5 us -> 91 us (0.924)
  the two profiles are of different devices: /device:TPU:6 before, /device:TPU:8 now
where the time goes in v1:
time: 91 us; the launch traced here: 90.7 us
  starting transfers between devices  41.1 us (45%)
  waiting for transfers between devices  28.3 us (31%)
  Pallas kernels  17.9 us (20%)
  local copies, waits for them, and re-layouts  2.04 us (2%)
  other arithmetic  1.1 us (1%)
    ppermute x31, starting transfers between devices, move(): return lax.ppermute(array, 'ctx', pairs)  41.1 us
    ppermute x31, waiting for transfers between devices, move(): return lax.ppermute(array, 'ctx', pairs)  28.3 us
    pallas_call x5, Pallas kernels, part(): pl.pallas_call(functools.partial(part_kernel, heads, groups), in_specs=[s...  10.9 us
    pallas_call x2, Pallas kernels, make_lists(): pl.pallas_call(functools.partial(list_kernel, first, spec), in_specs=[sme...  5.21 us
  transfers between devices with their start and end apart: 31, of which 10 were waited for; matrix products, arithmetic and copies ran while one was open for 1% of the time, Pallas kernels for 17%

profile of v1, /device:TPU:8, one launch (start us, length us, event | category | flops | bytes accessed | tf_op | source)
XLA Modules:
  0.0 90.7 jit_solution(8921517176809651073)
XLA Ops:
  0.0 0.7 fusion.1
  0.7 0.1 pad_maximum_fusion.2
  0.8 0.1 copy.10
  0.9 1.1 %fusion.4 = (bf16[128,640]{1,0:T(8,128)(2,1)S(1)}, bf16[128,640]{1,0:T(8,128)(2,1)S(1)}) fusion(bf16[256,640]{1,0:T(8,128)(2,1)} %param.5), kind=kLoop, calls=%fused_computation.28 | loop fusion | bytes 655360 | tf_op jit(solution)/shard_map/slice | solution.py:390
  2.0 0.0 copy-start.1
  2.0 2.0 %collective-permute-start.4 = (bf16[272,640]{1,0:T(8,128)(2,1)S(1)}, bf16[272,640]{1,0:T(8,128)(2,1)S(1)}, u32[]{:S(2)}, u32[]{:S(2)}) collective-permute-start(bf16[272,640]{1,0:T(8,128)(2,1)S(1)} %pad_maximum_fusion.1.rest_16_), channel_id=1, source_target_pairs={{0,8},{4,12},{8,16},{12,20},{16,24},{20,28},{24,32},{28,36},{32,40... | collective-permute-start | bytes 1044488 | tf_op jit(solution)/shard_map/ppermute | solution.py:38
  4.0 4.0 %collective-permute-start.5 = (bf16[272,640]{1,0:T(8,128)(2,1)S(1)}, bf16[272,640]{1,0:T(8,128)(2,1)}, u32[]{:S(2)}, u32[]{:S(2)}) collective-permute-start(bf16[272,640]{1,0:T(8,128)(2,1)S(1)} %pad_maximum_fusion.1.rest_16_), channel_id=1, source_target_pairs={{0,56},{4,60},{8,0},{12,4},{16,8},{20,12},{24,16},{28,20},{32,24},... | collective-permute-start | bytes 1044488 | tf_op jit(solution)/shard_map/ppermute | solution.py:38
  8.0 0.1 convert_reduce_fusion
  8.1 0.1 convert_reduce_fusion.1
  8.2 0.1 pad_maximum_fusion.refs_0_.rest_0_.rest_8_
  8.3 1.6 %collective-permute-start = (bf16[528,640]{1,0:T(8,128)(2,1)S(1)}, bf16[528,640]{1,0:T(8,128)(2,1)S(1)}, u32[]{:S(2)}, u32[]{:S(2)}) collective-permute-start(bf16[528,640]{1,0:T(8,128)(2,1)S(1)} %pad_maximum_fusion.refs_0_.rest_0_.rest_8_), channel_id=1, source_target_pairs={{0,64},{4,68},{8,72},{12,76},{16,80},{20,84},{24,88},{28,92},{32,9... | collective-permute-start | bytes 2027528 | tf_op jit(solution)/shard_map/ppermute | solution.py:38
  9.9 1.7 %collective-permute-start.2 = (bf16[528,640]{1,0:T(8,128)(2,1)S(1)}, bf16[528,640]{1,0:T(8,128)(2,1)S(1)}, u32[]{:S(2)}, u32[]{:S(2)}) collective-permute-start(bf16[528,640]{1,0:T(8,128)(2,1)S(1)} %pad_maximum_fusion.refs_0_.rest_0_.rest_8_), channel_id=1, source_target_pairs={{0,192},{4,196},{8,200},{12,204},{16,208},{20,212},{24,216},{28,22... | collective-permute-start | bytes 2027528 | tf_op jit(solution)/shard_map/ppermute | solution.py:38
  11.6 0.1 pad_add_fusion.pos_ref
  11.7 4.4 %collective-permute-done.4.rest_16_ = bf16[272,640]{1,0:T(8,128)(2,1)S(1)} collective-permute-done((bf16[272,640]{1,0:T(8,128)(2,1)S(1)}, bf16[272,640]{1,0:T(8,128)(2,1)S(1)}, u32[]{:S(2)}, u32[]{:S(2)}) %collective-permute-start.4) | collective-permute-done | bytes 348192 | tf_op jit(solution)/shard_map/ppermute | solution.py:38
  16.1 0.0 collective-permute-start.6
  16.1 0.0 collective-permute-done.5.rest_17_
  16.1 3.2 %collective-permute-start.7 = (bf16[272,640]{1,0:T(8,128)(2,1)}, bf16[272,640]{1,0:T(8,128)(2,1)S(1)}, u32[]{:S(2)}, u32[]{:S(2)}) collective-permute-start(bf16[272,640]{1,0:T(8,128)(2,1)} %collective-permute-done.5.rest_17_), channel_id=1, source_target_pairs={{0,56},{4,60},{8,0},{12,4},{16,8},{20,12},{24,16},{28,20},{32,24},... | collective-permute-start | bytes 1044488 | tf_op jit(solution)/shard_map/ppermute | solution.py:38
  19.3 0.7 constant_dynamic-update-slice_fusion.4
  20.1 6.2 %collective-permute-done.refs_6_.rest_6_.rest_14_ = bf16[528,640]{1,0:T(8,128)(2,1)S(1)} collective-permute-done((bf16[528,640]{1,0:T(8,128)(2,1)S(1)}, bf16[528,640]{1,0:T(8,128)(2,1)S(1)}, u32[]{:S(2)}, u32[]{:S(2)}) %collective-permute-start) | collective-permute-done | bytes 675872 | tf_op jit(solution)/shard_map/ppermute | solution.py:38
  26.3 0.4 collective-permute-start.1
  26.6 0.0 collective-permute-done.2.refs_2_.rest_2_.rest_10_
  26.7 3.0 %collective-permute-start.3 = (bf16[256,640]{1,0:T(8,128)(2,1)S(1)}, bf16[256,640]{1,0:T(8,128)(2,1)S(1)}, u32[]{:S(2)}, u32[]{:S(2)}) collective-permute-start(bf16[256,640]{1,0:T(8,128)(2,1)S(1)} %slice.53), channel_id=1, source_target_pairs={{0,192},{4,196},{8,200},{12,204},{16,208},{20,212},{24,216},{28,22... | collective-permute-start | bytes 983048 | tf_op jit(solution)/shard_map/ppermute | solution.py:38
  29.7 0.0 collective-permute-done.6.rest_16_
  29.7 3.2 %collective-permute-start.9 = (bf16[272,640]{1,0:T(8,128)(2,1)S(1)}, bf16[272,640]{1,0:T(8,128)(2,1)S(1)}, u32[]{:S(2)}, u32[]{:S(2)}) collective-permute-start(bf16[272,640]{1,0:T(8,128)(2,1)S(1)} %collective-permute-done.7.rest_17_), channel_id=1, source_target_pairs={{0,56},{4,60},{8,0},{12,4},{16,8},{20,12},{24,16},{28,20},{32,24},... | collective-permute-start | bytes 1044488 | tf_op jit(solution)/shard_map/ppermute | solution.py:38
  32.9 6.1 %collective-permute-done.8.rest_16_ = bf16[272,640]{1,0:T(8,128)(2,1)S(1)} collective-permute-done((bf16[272,640]{1,0:T(8,128)(2,1)S(1)}, bf16[272,640]{1,0:T(8,128)(2,1)S(1)}, u32[]{:S(2)}, u32[]{:S(2)}) %collective-permute-start.8) | collective-permute-done | bytes 348192 | tf_op jit(solution)/shard_map/ppermute | solution.py:38
  39.0 0.0 collective-permute-done.9.rest_17_
  39.0 0.5 collective-permute-start.13
  39.6 0.1 collective-permute-start.15
  39.7 3.2 %collective-permute-start.16 = (bf16[144,640]{1,0:T(8,128)(2,1)S(1)}, bf16[144,640]{1,0:T(8,128)(2,1)S(1)}, u32[]{:S(2)}, u32[]{:S(2)}) collective-permute-start(bf16[144,640]{1,0:T(8,128)(2,1)S(1)} %slice.61), channel_id=1, source_target_pairs={{0,56},{4,60},{8,0},{12,4},{16,8},{20,12},{24,16},{28,20},{32,24},... | collective-permute-start | bytes 552968 | tf_op jit(solution)/shard_map/ppermute | solution.py:38
  42.9 3.3 %shard_map.55 = (f32[7,64,256]{2,1,0:T(8,128)S(1)}, s32[7,128]{1,0:T(8,128)S(1)}) custom-call(s32[3]{0:T(128)S(1)} %pad_add_fusion.pos_ref, bf16[112,128]{1,0:T(8,128)(2,1)S(1)} %constant_dynamic-update-slice_fusion.asked_ref), custom_call_target="tpu_custom_call" | custom-call | flops 1000000 | bytes 1048576 | tf_op jit(solution)/shard_map/pallas_call | solution.py:95
  46.3 1.2 %collective-permute-done.15.asked_ref.rest_16_ = bf16[144,640]{1,0:T(8,128)(2,1)S(1)} collective-permute-done((bf16[144,640]{1,0:T(8,128)(2,1)S(1)}, bf16[144,640]{1,0:T(8,128)(2,1)S(1)}, u32[]{:S(2)}, u32[]{:S(2)}) %collective-permute-start.15) | collective-permute-done | bytes 184352 | tf_op jit(solution)/shard_map/ppermute | solution.py:38
  47.5 0.5 collective-permute-start.14
  48.0 1.9 %shard_map.61 = (f32[1,64,256]{2,1,0:T(8,128)S(1)}, s32[2,128]{1,0:T(2,128)S(1)}) custom-call(s32[3]{0:T(128)S(1)} %pad_add_fusion.pos_ref, bf16[144,640]{1,0:T(8,128)(2,1)S(1)} %collective-permute-done.15.asked_ref.rest_16_), custom_call_target="tpu_custom_call" | custom-call | flops 1000000 | bytes 1048576 | tf_op jit(solution)/shard_map/pallas_call | solution.py:95
  49.9 0.0 collective-permute-done.10.refs_1_.rest_1_.rest_9_
  49.9 0.0 collective-permute-done.13.refs_7_.rest_7_.rest_15_
  49.9 0.0 collective-permute-done.12.refs_5_.rest_5_
  50.0 0.0 collective-permute-done.14.rest_13_
  50.0 1.6 %shard_map.62 = (bf16[672,128]{1,0:T(8,128)(2,1)S(1)}, bf16[672,128]{1,0:T(8,128)(2,1)S(1)}) custom-call(s32[2,128]{1,0:T(2,128)S(1)} %get-tuple-element.60.list_ref, bf16[64,640]{1,0:T(8,128)(2,1)S(1)} %get-tuple-element.47.mean_k_ref, bf16[64,640]{1,0:T(8,128)(2,1)S(1)} %get-tuple-element.48.mean_v_ref, f32[1,64,256]{2,1,0:T(8,128)S(1)} %get-tuple-element.61.bias_ref, ...), custom_call_target="tpu_custom_call" | custom-call | flops 1342177280 | bytes 4194304 | tf_op jit(solution)/shard_map/pallas_call | solution.py:306
  51.6 2.8 %collective-permute-start.17 = (bf16[672,128]{1,0:T(8,128)(2,1)S(1)}, bf16[672,128]{1,0:T(8,128)(2,1)S(1)}, u32[]{:S(2)}, u32[]{:S(2)}) collective-permute-start(bf16[672,128]{1,0:T(8,128)(2,1)S(1)} %get-tuple-element.63), channel_id=1, source_target_pairs={{0,56},{4,60},{8,0},{12,4},{16,8},{20,12},{24,16},{28,20},{32,24},... | collective-permute-start | bytes 516104 | tf_op jit(solution)/shard_map/ppermute | solution.py:38
  54.4 2.7 %shard_map.60 = (bf16[672,128]{1,0:T(8,128)(2,1)S(1)}, bf16[672,128]{1,0:T(8,128)(2,1)S(1)}, bf16[672,128]{1,0:T(8,128)(2,1)S(1)}, bf16[672,128]{1,0:T(8,128)(2,1)S(1)}) custom-call(s32[7,128]{1,0:T(8,128)S(1)} %get-tuple-element.45.list_ref, bf16[64,640]{1,0:T(8,128)(2,1)S(1)} %get-tuple-element.47.mean_k_ref, ...), custom_call_target="tpu_custom_call" | custom-call | flops 1342177280 | bytes 4194304 | tf_op jit(solution)/shard_map/pallas_call | solution.py:306
  57.1 2.5 %collective-permute-start.24 = (bf16[672,128]{1,0:T(8,128)(2,1)S(1)}, bf16[672,128]{1,0:T(8,128)(2,1)S(1)}, u32[]{:S(2)}, u32[]{:S(2)}) collective-permute-start(bf16[672,128]{1,0:T(8,128)(2,1)S(1)} %get-tuple-element.74), channel_id=1, source_target_pairs={{0,56},{4,60},{8,0},{12,4},{16,8},{20,12},{24,16},{28,20},{32,24},... | collective-permute-start | bytes 516104 | tf_op jit(solution)/shard_map/ppermute | solution.py:38
  59.6 2.4 %collective-permute-done.18.refs_3_ = bf16[672,128]{1,0:T(8,128)(2,1)S(1)} collective-permute-done((bf16[672,128]{1,0:T(8,128)(2,1)S(1)}, bf16[672,128]{1,0:T(8,128)(2,1)S(1)}, u32[]{:S(2)}, u32[]{:S(2)}) %collective-permute-start.18) | collective-permute-done | bytes 172064 | tf_op jit(solution)/shard_map/ppermute | solution.py:38
  62.1 0.1 shard_map.63
  62.2 0.9 collective-permute-start.19
  63.1 1.2 %collective-permute-start.20 = (bf16[672,128]{1,0:T(8,128)(2,1)S(1)}, bf16[672,128]{1,0:T(8,128)(2,1)S(1)}, u32[]{:S(2)}, u32[]{:S(2)}) collective-permute-start(bf16[672,128]{1,0:T(8,128)(2,1)S(1)} %get-tuple-element.66), channel_id=1, source_target_pairs={{0,8},{4,12},{8,16},{12,20},{16,24},{20,28},{24,32},{28,36},{32,40... | collective-permute-start | bytes 516104 | tf_op jit(solution)/shard_map/ppermute | solution.py:38
  64.3 2.9 %shard_map.59 = (bf16[672,128]{1,0:T(8,128)(2,1)S(1)}, bf16[672,128]{1,0:T(8,128)(2,1)S(1)}, bf16[672,128]{1,0:T(8,128)(2,1)S(1)}, bf16[672,128]{1,0:T(8,128)(2,1)S(1)}) custom-call(s32[7,128]{1,0:T(8,128)S(1)} %get-tuple-element.45.list_ref, bf16[64,640]{1,0:T(8,128)(2,1)S(1)} %get-tuple-element.47.mean_k_ref, ...), custom_call_target="tpu_custom_call" | custom-call | flops 1342177280 | bytes 4194304 | tf_op jit(solution)/shard_map/pallas_call | solution.py:306
  67.3 0.1 collective-permute-done.25.refs_3_
  67.4 0.1 shard_map.66
  67.6 1.1 %collective-permute-start.26 = (bf16[672,128]{1,0:T(8,128)(2,1)S(1)}, bf16[672,128]{1,0:T(8,128)(2,1)S(1)}, u32[]{:S(2)}, u32[]{:S(2)}) collective-permute-start(bf16[672,128]{1,0:T(8,128)(2,1)S(1)} %get-tuple-element.76), channel_id=1, source_target_pairs={{0,56},{4,60},{8,0},{12,4},{16,8},{20,12},{24,16},{28,20},{32,24},... | collective-permute-start | bytes 516104 | tf_op jit(solution)/shard_map/ppermute | solution.py:38
  68.7 1.0 %collective-permute-start.27 = (bf16[672,128]{1,0:T(8,128)(2,1)S(1)}, bf16[672,128]{1,0:T(8,128)(2,1)S(1)}, u32[]{:S(2)}, u32[]{:S(2)}) collective-permute-start(bf16[672,128]{1,0:T(8,128)(2,1)S(1)} %get-tuple-element.77), channel_id=1, source_target_pairs={{0,8},{4,12},{8,16},{12,20},{16,24},{20,28},{24,32},{28,36},{32,40... | collective-permute-start | bytes 516104 | tf_op jit(solution)/shard_map/ppermute | solution.py:38
  69.7 0.7 collective-permute-done.20.refs_3_
  70.4 0.1 shard_map.64
  70.6 1.6 %collective-permute-start.21 = (bf16[672,128]{1,0:T(8,128)(2,1)S(1)}, bf16[672,128]{1,0:T(8,128)(2,1)S(1)}, u32[]{:S(2)}, u32[]{:S(2)}) collective-permute-start(bf16[672,128]{1,0:T(8,128)(2,1)S(1)} %get-tuple-element.67), channel_id=1, source_target_pairs={{0,56},{4,60},{8,0},{12,4},{16,8},{20,12},{24,16},{28,20},{32,24},... | collective-permute-start | bytes 516104 | tf_op jit(solution)/shard_map/ppermute | solution.py:38
  72.2 0.5 collective-permute-start.22
  72.7 2.3 %shard_map.58 = (bf16[672,128]{1,0:T(8,128)(2,1)S(1)}, bf16[672,128]{1,0:T(8,128)(2,1)S(1)}, bf16[672,128]{1,0:T(8,128)(2,1)S(1)}, bf16[672,128]{1,0:T(8,128)(2,1)S(1)}) custom-call(s32[7,128]{1,0:T(8,128)S(1)} %get-tuple-element.45.list_ref, bf16[64,640]{1,0:T(8,128)(2,1)S(1)} %get-tuple-element.47.mean_k_ref, ...), custom_call_target="tpu_custom_call" | custom-call | flops 1342177280 | bytes 4194304 | tf_op jit(solution)/shard_map/pallas_call | solution.py:306
  75.0 1.8 %collective-permute-done.27.refs_3_ = bf16[672,128]{1,0:T(8,128)(2,1)S(1)} collective-permute-done((bf16[672,128]{1,0:T(8,128)(2,1)S(1)}, bf16[672,128]{1,0:T(8,128)(2,1)S(1)}, u32[]{:S(2)}, u32[]{:S(2)}) %collective-permute-start.27) | collective-permute-done | bytes 172064 | tf_op jit(solution)/shard_map/ppermute | solution.py:38
  76.8 0.1 shard_map.67
  77.0 2.6 %collective-permute-start.28 = (bf16[672,128]{1,0:T(8,128)(2,1)S(1)}, bf16[672,128]{1,0:T(8,128)(2,1)S(1)}, u32[]{:S(2)}, u32[]{:S(2)}) collective-permute-start(bf16[672,128]{1,0:T(8,128)(2,1)S(1)} %get-tuple-element.78), channel_id=1, source_target_pairs={{0,56},{4,60},{8,0},{12,4},{16,8},{20,12},{24,16},{28,20},{32,24},... | collective-permute-start | bytes 516104 | tf_op jit(solution)/shard_map/ppermute | solution.py:38
  79.6 0.2 shard_map.65
  79.7 3.3 %collective-permute-start.23 = (bf16[672,128]{1,0:T(8,128)(2,1)S(1)}, bf16[672,128]{1,0:T(8,128)(2,1)S(1)}, u32[]{:S(2)}, u32[]{:S(2)}) collective-permute-start(bf16[672,128]{1,0:T(8,128)(2,1)S(1)} %get-tuple-element.69), channel_id=1, source_target_pairs={{0,56},{4,60},{8,0},{12,4},{16,8},{20,12},{24,16},{28,20},{32,24},... | collective-permute-start | bytes 516104 | tf_op jit(solution)/shard_map/ppermute | solution.py:38
  83.1 1.3 %shard_map.57 = (bf16[672,128]{1,0:T(8,128)(2,1)S(1)}, bf16[672,128]{1,0:T(8,128)(2,1)S(1)}) custom-call(s32[7,128]{1,0:T(8,128)S(1)} %get-tuple-element.45.list_ref, bf16[64,640]{1,0:T(8,128)(2,1)S(1)} %get-tuple-element.47.mean_k_ref, bf16[64,640]{1,0:T(8,128)(2,1)S(1)} %get-tuple-element.48.mean_v_ref, f32[7,64,256]{2,1,0:T(8,128)S(1)} %get-tuple-element.49.bias_ref, ...), custom_call_target="tpu_custom_call" | custom-call | flops 1342177280 | bytes 4194304 | tf_op jit(solution)/shard_map/pallas_call | solution.py:306
  84.4 2.9 %collective-permute-done.29.refs_4_ = bf16[672,128]{1,0:T(8,128)(2,1)S(1)} collective-permute-done((bf16[672,128]{1,0:T(8,128)(2,1)S(1)}, bf16[672,128]{1,0:T(8,128)(2,1)S(1)}, u32[]{:S(2)}, u32[]{:S(2)}) %collective-permute-start.29) | collective-permute-done | bytes 172064 | tf_op jit(solution)/shard_map/ppermute | solution.py:38
  87.4 2.3 %collective-permute-done.30.refs_5_ = bf16[672,128]{1,0:T(8,128)(2,1)S(1)} collective-permute-done((bf16[672,128]{1,0:T(8,128)(2,1)S(1)}, bf16[672,128]{1,0:T(8,128)(2,1)S(1)}, u32[]{:S(2)}, u32[]{:S(2)}) %collective-permute-start.30) | collective-permute-done | bytes 172064 | tf_op jit(solution)/shard_map/ppermute | solution.py:38
  89.7 1.0 %shard_map.68 = bf16[256,640]{1,0:T(8,128)(2,1)} custom-call(bf16[672,128]{1,0:T(8,128)(2,1)S(1)} %get-tuple-element.51.refs_0_, bf16[672,128]{1,0:T(8,128)(2,1)S(1)} %get-tuple-element.52.refs_1_, bf16[672,128]{1,0:T(8,128)(2,1)S(1)} %collective-permute-done.23.refs_2_, bf16[672,128]{1,0:T(8,128)(2,1)S(1)} %collective-permute-done.28.refs_3_, ...), custom_call_target="tpu_custom_call" | custom-call | tf_op jit(solution)/shard_map/pallas_call | solution.py:370
  (38 shorter events, 0.3 us)
Async XLA Ops:
  0.9 7.2 %copy-start = (bf16[256,640]{1,0:T(8,128)(2,1)S(1)}, bf16[256,640]{1,0:T(8,128)(2,1)}, u32[]{:S(2)}) copy-start(bf16[256,640]{1,0:T(8,128)(2,1)} %param.7) | copy-start | bytes 983044
  2.0 6.2 %copy-start.1 = (bf16[256,640]{1,0:T(8,128)(2,1)S(1)}, bf16[256,640]{1,0:T(8,128)(2,1)}, u32[]{:S(2)}) copy-start(bf16[256,640]{1,0:T(8,128)(2,1)} %param.6) | copy-start | bytes 983044
  2.0 14.1 %collective-permute-start.4 = (bf16[272,640]{1,0:T(8,128)(2,1)S(1)}, bf16[272,640]{1,0:T(8,128)(2,1)S(1)}, u32[]{:S(2)}, u32[]{:S(2)}) collective-permute-start(bf16[272,640]{1,0:T(8,128)(2,1)S(1)} %pad_maximum_fusion.1.rest_16_), channel_id=1, source_target_pairs={{0,8},{4,12},{8,16},{12,20},{16,24},{20,28},{24,32},{28,36},{32,40... | collective-permute-start | bytes 1044488 | tf_op jit(solution)/shard_map/ppermute | solution.py:38
  4.0 12.1 %collective-permute-start.5 = (bf16[272,640]{1,0:T(8,128)(2,1)S(1)}, bf16[272,640]{1,0:T(8,128)(2,1)}, u32[]{:S(2)}, u32[]{:S(2)}) collective-permute-start(bf16[272,640]{1,0:T(8,128)(2,1)S(1)} %pad_maximum_fusion.1.rest_16_), channel_id=1, source_target_pairs={{0,56},{4,60},{8,0},{12,4},{16,8},{20,12},{24,16},{28,20},{32,24},... | collective-permute-start | bytes 1044488 | tf_op jit(solution)/shard_map/ppermute | solution.py:38
  8.3 17.9 %collective-permute-start = (bf16[528,640]{1,0:T(8,128)(2,1)S(1)}, bf16[528,640]{1,0:T(8,128)(2,1)S(1)}, u32[]{:S(2)}, u32[]{:S(2)}) collective-permute-start(bf16[528,640]{1,0:T(8,128)(2,1)S(1)} %pad_maximum_fusion.refs_0_.rest_0_.rest_8_), channel_id=1, source_target_pairs={{0,64},{4,68},{8,72},{12,76},{16,80},{20,84},{24,88},{28,92},{32,9... | collective-permute-start | bytes 2027528 | tf_op jit(solution)/shard_map/ppermute | solution.py:38
  9.9 16.7 %collective-permute-start.2 = (bf16[528,640]{1,0:T(8,128)(2,1)S(1)}, bf16[528,640]{1,0:T(8,128)(2,1)S(1)}, u32[]{:S(2)}, u32[]{:S(2)}) collective-permute-start(bf16[528,640]{1,0:T(8,128)(2,1)S(1)} %pad_maximum_fusion.refs_0_.rest_0_.rest_8_), channel_id=1, source_target_pairs={{0,192},{4,196},{8,200},{12,204},{16,208},{20,212},{24,216},{28,22... | collective-permute-start | bytes 2027528 | tf_op jit(solution)/shard_map/ppermute | solution.py:38
  11.6 38.3 %collective-permute-start.10 = (bf16[528,640]{1,0:T(8,128)(2,1)S(1)}, bf16[528,640]{1,0:T(8,128)(2,1)S(1)}, u32[]{:S(2)}, u32[]{:S(2)}) collective-permute-start(bf16[528,640]{1,0:T(8,128)(2,1)S(1)} %pad_maximum_fusion.refs_0_.rest_0_.rest_8_), channel_id=1, source_target_pairs={{0,4},{4,0},{8,12},{12,8},{16,20},{20,16},{24,28},{28,24},{32,36},... | collective-permute-start | bytes 2027528 | tf_op jit(solution)/shard_map/ppermute | solution.py:38
  16.1 13.6 %collective-permute-start.6 = (bf16[272,640]{1,0:T(8,128)(2,1)S(1)}, bf16[272,640]{1,0:T(8,128)(2,1)S(1)}, u32[]{:S(2)}, u32[]{:S(2)}) collective-permute-start(bf16[272,640]{1,0:T(8,128)(2,1)S(1)} %collective-permute-done.4.rest_16_), channel_id=1, source_target_pairs={{0,8},{4,12},{8,16},{12,20},{16,24},{20,28},{24,32},{28,36},{32,40... | collective-permute-start | bytes 1044488 | tf_op jit(solution)/shard_map/ppermute | solution.py:38
  16.1 13.6 %collective-permute-start.7 = (bf16[272,640]{1,0:T(8,128)(2,1)}, bf16[272,640]{1,0:T(8,128)(2,1)S(1)}, u32[]{:S(2)}, u32[]{:S(2)}) collective-permute-start(bf16[272,640]{1,0:T(8,128)(2,1)} %collective-permute-done.5.rest_17_), channel_id=1, source_target_pairs={{0,56},{4,60},{8,0},{12,4},{16,8},{20,12},{24,16},{28,20},{32,24},... | collective-permute-start | bytes 1044488 | tf_op jit(solution)/shard_map/ppermute | solution.py:38
  26.3 13.5 %collective-permute-start.1 = (bf16[272,640]{1,0:T(8,128)(2,1)S(1)}, bf16[272,640]{1,0:T(8,128)(2,1)S(1)}, u32[]{:S(2)}, u32[]{:S(2)}) collective-permute-start(bf16[272,640]{1,0:T(8,128)(2,1)S(1)} %slice.52), channel_id=1, source_target_pairs={{0,64},{4,68},{8,72},{12,76},{16,80},{20,84},{24,88},{28,92},{32,9... | collective-permute-start | bytes 1044488 | tf_op jit(solution)/shard_map/ppermute | solution.py:38
  26.7 13.0 %collective-permute-start.3 = (bf16[256,640]{1,0:T(8,128)(2,1)S(1)}, bf16[256,640]{1,0:T(8,128)(2,1)S(1)}, u32[]{:S(2)}, u32[]{:S(2)}) collective-permute-start(bf16[256,640]{1,0:T(8,128)(2,1)S(1)} %slice.53), channel_id=1, source_target_pairs={{0,192},{4,196},{8,200},{12,204},{16,208},{20,212},{24,216},{28,22... | collective-permute-start | bytes 983048 | tf_op jit(solution)/shard_map/ppermute | solution.py:38
  29.7 9.4 %collective-permute-start.8 = (bf16[272,640]{1,0:T(8,128)(2,1)S(1)}, bf16[272,640]{1,0:T(8,128)(2,1)S(1)}, u32[]{:S(2)}, u32[]{:S(2)}) collective-permute-start(bf16[272,640]{1,0:T(8,128)(2,1)S(1)} %collective-permute-done.6.rest_16_), channel_id=1, source_target_pairs={{0,8},{4,12},{8,16},{12,20},{16,24},{20,28},{24,32},{28,36},{32,40... | collective-permute-start | bytes 1044488 | tf_op jit(solution)/shard_map/ppermute | solution.py:38
  29.7 9.3 %collective-permute-start.9 = (bf16[272,640]{1,0:T(8,128)(2,1)S(1)}, bf16[272,640]{1,0:T(8,128)(2,1)S(1)}, u32[]{:S(2)}, u32[]{:S(2)}) collective-permute-start(bf16[272,640]{1,0:T(8,128)(2,1)S(1)} %collective-permute-done.7.rest_17_), channel_id=1, source_target_pairs={{0,56},{4,60},{8,0},{12,4},{16,8},{20,12},{24,16},{28,20},{32,24},... | collective-permute-start | bytes 1044488 | tf_op jit(solution)/shard_map/ppermute | solution.py:38
  39.0 10.9 %collective-permute-start.11 = (bf16[528,640]{1,0:T(8,128)(2,1)S(1)}, bf16[528,640]{1,0:T(8,128)(2,1)S(1)}, u32[]{:S(2)}, u32[]{:S(2)}) collective-permute-start(bf16[528,640]{1,0:T(8,128)(2,1)S(1)} %collective-permute-done.2.refs_2_.rest_2_.rest_10_), channel_id=1, source_target_pairs={{0,4},{4,0},{8,12},{12,8},{16,20},{20,16},{24,28},{28,24},{32,36},... | collective-permute-start | bytes 2027528 | tf_op jit(solution)/shard_map/ppermute | solution.py:38
  39.0 10.9 %collective-permute-start.13 = (bf16[528,640]{1,0:T(8,128)(2,1)S(1)}, bf16[528,640]{1,0:T(8,128)(2,1)S(1)}, u32[]{:S(2)}, u32[]{:S(2)}) collective-permute-start(bf16[528,640]{1,0:T(8,128)(2,1)S(1)} %collective-permute-done.refs_6_.rest_6_.rest_14_), channel_id=1, source_target_pairs={{0,4},{4,0},{8,12},{12,8},{16,20},{20,16},{24,28},{28,24},{32,36},... | collective-permute-start | bytes 2027528 | tf_op jit(solution)/shard_map/ppermute | solution.py:38
  39.6 7.8 %collective-permute-start.15 = (bf16[144,640]{1,0:T(8,128)(2,1)S(1)}, bf16[144,640]{1,0:T(8,128)(2,1)S(1)}, u32[]{:S(2)}, u32[]{:S(2)}) collective-permute-start(bf16[144,640]{1,0:T(8,128)(2,1)S(1)} %slice.60), channel_id=1, source_target_pairs={{0,8},{4,12},{8,16},{12,20},{16,24},{20,28},{24,32},{28,36},{32,40... | collective-permute-start | bytes 552968 | tf_op jit(solution)/shard_map/ppermute | solution.py:38
  39.7 7.7 %collective-permute-start.16 = (bf16[144,640]{1,0:T(8,128)(2,1)S(1)}, bf16[144,640]{1,0:T(8,128)(2,1)S(1)}, u32[]{:S(2)}, u32[]{:S(2)}) collective-permute-start(bf16[144,640]{1,0:T(8,128)(2,1)S(1)} %slice.61), channel_id=1, source_target_pairs={{0,56},{4,60},{8,0},{12,4},{16,8},{20,12},{24,16},{28,20},{32,24},... | collective-permute-start | bytes 552968 | tf_op jit(solution)/shard_map/ppermute | solution.py:38
  47.5 2.5 %collective-permute-start.12 = (bf16[272,640]{1,0:T(8,128)(2,1)S(1)}, bf16[272,640]{1,0:T(8,128)(2,1)S(1)}, u32[]{:S(2)}, u32[]{:S(2)}) collective-permute-start(bf16[272,640]{1,0:T(8,128)(2,1)S(1)} %collective-permute-done.1.refs_4_.rest_4_), channel_id=1, source_target_pairs={{0,4},{4,0},{8,12},{12,8},{16,20},{20,16},{24,28},{28,24},{32,36},... | collective-permute-start | bytes 1044488 | tf_op jit(solution)/shard_map/ppermute | solution.py:38
  47.5 2.5 %collective-permute-start.14 = (bf16[256,640]{1,0:T(8,128)(2,1)S(1)}, bf16[256,640]{1,0:T(8,128)(2,1)S(1)}, u32[]{:S(2)}, u32[]{:S(2)}) collective-permute-start(bf16[256,640]{1,0:T(8,128)(2,1)S(1)} %collective-permute-done.3.rest_12_), channel_id=1, source_target_pairs={{0,4},{4,0},{8,12},{12,8},{16,20},{20,16},{24,28},{28,24},{32,36},... | collective-permute-start | bytes 983048 | tf_op jit(solution)/shard_map/ppermute | solution.py:38
  51.6 8.0 %collective-permute-start.17 = (bf16[672,128]{1,0:T(8,128)(2,1)S(1)}, bf16[672,128]{1,0:T(8,128)(2,1)S(1)}, u32[]{:S(2)}, u32[]{:S(2)}) collective-permute-start(bf16[672,128]{1,0:T(8,128)(2,1)S(1)} %get-tuple-element.63), channel_id=1, source_target_pairs={{0,56},{4,60},{8,0},{12,4},{16,8},{20,12},{24,16},{28,20},{32,24},... | collective-permute-start | bytes 516104 | tf_op jit(solution)/shard_map/ppermute | solution.py:38
  54.4 7.7 %collective-permute-start.18 = (bf16[672,128]{1,0:T(8,128)(2,1)S(1)}, bf16[672,128]{1,0:T(8,128)(2,1)S(1)}, u32[]{:S(2)}, u32[]{:S(2)}) collective-permute-start(bf16[672,128]{1,0:T(8,128)(2,1)S(1)} %get-tuple-element.64), channel_id=1, source_target_pairs={{0,8},{4,12},{8,16},{12,20},{16,24},{20,28},{24,32},{28,36},{32,40... | collective-permute-start | bytes 516104 | tf_op jit(solution)/shard_map/ppermute | solution.py:38
  57.1 10.2 %collective-permute-start.24 = (bf16[672,128]{1,0:T(8,128)(2,1)S(1)}, bf16[672,128]{1,0:T(8,128)(2,1)S(1)}, u32[]{:S(2)}, u32[]{:S(2)}) collective-permute-start(bf16[672,128]{1,0:T(8,128)(2,1)S(1)} %get-tuple-element.74), channel_id=1, source_target_pairs={{0,56},{4,60},{8,0},{12,4},{16,8},{20,12},{24,16},{28,20},{32,24},... | collective-permute-start | bytes 516104 | tf_op jit(solution)/shard_map/ppermute | solution.py:38
  59.6 7.8 %collective-permute-start.25 = (bf16[672,128]{1,0:T(8,128)(2,1)S(1)}, bf16[672,128]{1,0:T(8,128)(2,1)S(1)}, u32[]{:S(2)}, u32[]{:S(2)}) collective-permute-start(bf16[672,128]{1,0:T(8,128)(2,1)S(1)} %get-tuple-element.75), channel_id=1, source_target_pairs={{0,8},{4,12},{8,16},{12,20},{16,24},{20,28},{24,32},{28,36},{32,40... | collective-permute-start | bytes 516104 | tf_op jit(solution)/shard_map/ppermute | solution.py:38
  62.2 7.5 %collective-permute-start.19 = (bf16[672,128]{1,0:T(8,128)(2,1)S(1)}, bf16[672,128]{1,0:T(8,128)(2,1)S(1)}, u32[]{:S(2)}, u32[]{:S(2)}) collective-permute-start(bf16[672,128]{1,0:T(8,128)(2,1)S(1)} %get-tuple-element.65), channel_id=1, source_target_pairs={{0,56},{4,60},{8,0},{12,4},{16,8},{20,12},{24,16},{28,20},{32,24},... | collective-permute-start | bytes 516104 | tf_op jit(solution)/shard_map/ppermute | solution.py:38
  63.1 7.3 %collective-permute-start.20 = (bf16[672,128]{1,0:T(8,128)(2,1)S(1)}, bf16[672,128]{1,0:T(8,128)(2,1)S(1)}, u32[]{:S(2)}, u32[]{:S(2)}) collective-permute-start(bf16[672,128]{1,0:T(8,128)(2,1)S(1)} %get-tuple-element.66), channel_id=1, source_target_pairs={{0,8},{4,12},{8,16},{12,20},{16,24},{20,28},{24,32},{28,36},{32,40... | collective-permute-start | bytes 516104 | tf_op jit(solution)/shard_map/ppermute | solution.py:38
  67.6 7.4 %collective-permute-start.26 = (bf16[672,128]{1,0:T(8,128)(2,1)S(1)}, bf16[672,128]{1,0:T(8,128)(2,1)S(1)}, u32[]{:S(2)}, u32[]{:S(2)}) collective-permute-start(bf16[672,128]{1,0:T(8,128)(2,1)S(1)} %get-tuple-element.76), channel_id=1, source_target_pairs={{0,56},{4,60},{8,0},{12,4},{16,8},{20,12},{24,16},{28,20},{32,24},... | collective-permute-start | bytes 516104 | tf_op jit(solution)/shard_map/ppermute | solution.py:38
  68.7 8.1 %collective-permute-start.27 = (bf16[672,128]{1,0:T(8,128)(2,1)S(1)}, bf16[672,128]{1,0:T(8,128)(2,1)S(1)}, u32[]{:S(2)}, u32[]{:S(2)}) collective-permute-start(bf16[672,128]{1,0:T(8,128)(2,1)S(1)} %get-tuple-element.77), channel_id=1, source_target_pairs={{0,8},{4,12},{8,16},{12,20},{16,24},{20,28},{24,32},{28,36},{32,40... | collective-permute-start | bytes 516104 | tf_op jit(solution)/shard_map/ppermute | solution.py:38
  70.6 9.0 %collective-permute-start.21 = (bf16[672,128]{1,0:T(8,128)(2,1)S(1)}, bf16[672,128]{1,0:T(8,128)(2,1)S(1)}, u32[]{:S(2)}, u32[]{:S(2)}) collective-permute-start(bf16[672,128]{1,0:T(8,128)(2,1)S(1)} %get-tuple-element.67), channel_id=1, source_target_pairs={{0,56},{4,60},{8,0},{12,4},{16,8},{20,12},{24,16},{28,20},{32,24},... | collective-permute-start | bytes 516104 | tf_op jit(solution)/shard_map/ppermute | solution.py:38
  72.2 7.4 %collective-permute-start.22 = (bf16[672,128]{1,0:T(8,128)(2,1)S(1)}, bf16[672,128]{1,0:T(8,128)(2,1)S(1)}, u32[]{:S(2)}, u32[]{:S(2)}) collective-permute-start(bf16[672,128]{1,0:T(8,128)(2,1)S(1)} %get-tuple-element.68), channel_id=1, source_target_pairs={{0,8},{4,12},{8,16},{12,20},{16,24},{20,28},{24,32},{28,36},{32,40... | collective-permute-start | bytes 516104 | tf_op jit(solution)/shard_map/ppermute | solution.py:38
  77.0 7.5 %collective-permute-start.28 = (bf16[672,128]{1,0:T(8,128)(2,1)S(1)}, bf16[672,128]{1,0:T(8,128)(2,1)S(1)}, u32[]{:S(2)}, u32[]{:S(2)}) collective-permute-start(bf16[672,128]{1,0:T(8,128)(2,1)S(1)} %get-tuple-element.78), channel_id=1, source_target_pairs={{0,56},{4,60},{8,0},{12,4},{16,8},{20,12},{24,16},{28,20},{32,24},... | collective-permute-start | bytes 516104 | tf_op jit(solution)/shard_map/ppermute | solution.py:38
  79.6 7.8 %collective-permute-start.29 = (bf16[672,128]{1,0:T(8,128)(2,1)S(1)}, bf16[672,128]{1,0:T(8,128)(2,1)S(1)}, u32[]{:S(2)}, u32[]{:S(2)}) collective-permute-start(bf16[672,128]{1,0:T(8,128)(2,1)S(1)} %get-tuple-element.79), channel_id=1, source_target_pairs={{0,8},{4,12},{8,16},{12,20},{16,24},{20,28},{24,32},{28,36},{32,40... | collective-permute-start | bytes 516104 | tf_op jit(solution)/shard_map/ppermute | solution.py:38
  79.7 7.6 %collective-permute-start.23 = (bf16[672,128]{1,0:T(8,128)(2,1)S(1)}, bf16[672,128]{1,0:T(8,128)(2,1)S(1)}, u32[]{:S(2)}, u32[]{:S(2)}) collective-permute-start(bf16[672,128]{1,0:T(8,128)(2,1)S(1)} %get-tuple-element.69), channel_id=1, source_target_pairs={{0,56},{4,60},{8,0},{12,4},{16,8},{20,12},{24,16},{28,20},{32,24},... | collective-permute-start | bytes 516104 | tf_op jit(solution)/shard_map/ppermute | solution.py:38
  83.1 6.6 %collective-permute-start.30 = (bf16[672,128]{1,0:T(8,128)(2,1)S(1)}, bf16[672,128]{1,0:T(8,128)(2,1)S(1)}, u32[]{:S(2)}, u32[]{:S(2)}) collective-permute-start(bf16[672,128]{1,0:T(8,128)(2,1)S(1)} %get-tuple-element.80), channel_id=1, source_target_pairs={{0,8},{4,12},{8,16},{12,20},{16,24},{20,28},{24,32},{28,36},{32,40... | collective-permute-start | bytes 516104 | tf_op jit(solution)/shard_map/ppermute | solution.py:38

commit v2 on v1

--- a/solution.py
+++ b/solution.py
@@ -20,7 +20,7 @@
 MEANS = 16
 PLANE = NX * NC
 MOST = 2 * PLANE
-FIRST = 2
+FIRST = 4
 CHUNK = 4
 NEGATIVE = -1e30
 ROWS_ROWS = (((1,), (1,)), ((), ()))
@@ -115,6 +115,16 @@
     tiles = [source[TOKENS : TOKENS + MEANS].astype(jnp.float32) for source in sources]
     mean_k_ref[...] = jnp.concatenate([t[:BLOCKS] for t in tiles], axis=0).astype(jnp.bfloat16)
     mean_v_ref[...] = jnp.concatenate([t[BLOCKS:] for t in tiles], axis=0).astype(jnp.bfloat16)
+
+
+def cut_kernel(up_ref, down_ref, up_out, down_out):
+    up_out[...] = up_ref[: HALF + REQUEST]
+    down_out[...] = down_ref[HALF:]
+
+
+def cut(up, down):
+    shape = jax.ShapeDtypeStruct((HALF + REQUEST, up.shape[1]), up.dtype)
+    return pl.pallas_call(cut_kernel, out_shape=(shape, shape), compiler_params=PARAMS)(up, down)
 
 
 def gather_means(sources):
@@ -404,8 +414,8 @@
     far_k, far_v = move(left[:split], dx=1), move(right[split:], dx=-1)
     left_twin, right_twin = move(left, dc=1), move(right, dc=1)
     up3, down3 = move(up2, dz=1), move(down2, dz=-1)
-    far_up = move(up3[: HALF + REQUEST], dz=1)
-    far_down = move(down3[HALF:], dz=-1)
+    far_up, far_down = cut(up3, down3)
+    far_up, far_down = move(far_up, dz=1), move(far_down, dz=-1)
     payloads = (pay, up1, down1, up2, down2, up3, down3)
     requests = [p[HALF : HALF + REQUEST, :HD] for p in payloads]
     tables = len(payloads)

time: 91 us -> 90.7 us (level)
  transfers between devices with their start and end apart: 31 -> 31, of which waited for: 10 -> 11; matrix products, arithmetic and copies ran while one was open for 1% -> 1% of each run, Pallas kernels for 17% -> 16%
where the time goes in v2:
time: 90.7 us; the launch traced here: 90.5 us
  starting transfers between devices  40.7 us (45%)
  waiting for transfers between devices  28.6 us (32%)
  Pallas kernels  17.8 us (20%)
  local copies, waits for them, and re-layouts  1.99 us (2%)
  other arithmetic  1.1 us (1%)
    ppermute x31, starting transfers between devices, move(): return lax.ppermute(array, 'ctx', pairs)  40.7 us
    ppermute x31, waiting for transfers between devices, move(): return lax.ppermute(array, 'ctx', pairs)  28.6 us
    pallas_call x5, Pallas kernels, part(): pl.pallas_call(functools.partial(part_kernel, heads, groups), in_specs=[s...  10.9 us
    pallas_call x2, Pallas kernels, make_lists(): pl.pallas_call(functools.partial(list_kernel, first, spec), in_specs=[sme...  5.09 us
  transfers between devices with their start and end apart: 31, of which 11 were waited for; matrix products, arithmetic and copies ran while one was open for 1% of the time, Pallas kernels for 16%

profile of v2, /device:TPU:8, one launch (start us, length us, event | category | flops | bytes accessed | tf_op | source)
XLA Modules:
  0.0 90.5 jit_solution(16698905433591134167)
XLA Ops:
  0.0 0.7 fusion.1
  0.7 0.1 pad_maximum_fusion.2
  0.8 0.1 copy.10
  0.9 1.1 %fusion.4 = (bf16[128,640]{1,0:T(8,128)(2,1)S(1)}, bf16[128,640]{1,0:T(8,128)(2,1)S(1)}) fusion(bf16[256,640]{1,0:T(8,128)(2,1)} %param.5), kind=kLoop, calls=%fused_computation.28 | loop fusion | bytes 655360 | tf_op jit(solution)/shard_map/slice | solution.py:400
  2.0 0.0 copy-start.1
  2.0 2.0 %collective-permute-start.4 = (bf16[272,640]{1,0:T(8,128)(2,1)S(1)}, bf16[272,640]{1,0:T(8,128)(2,1)S(1)}, u32[]{:S(2)}, u32[]{:S(2)}) collective-permute-start(bf16[272,640]{1,0:T(8,128)(2,1)S(1)} %pad_maximum_fusion.1.rest_16_), channel_id=1, source_target_pairs={{0,8},{4,12},{8,16},{12,20},{16,24},{20,28},{24,32},{28,36},{32,40... | collective-permute-start | bytes 1044488 | tf_op jit(solution)/shard_map/ppermute | solution.py:38
  4.0 4.0 %collective-permute-start.5 = (bf16[272,640]{1,0:T(8,128)(2,1)S(1)}, bf16[272,640]{1,0:T(8,128)(2,1)}, u32[]{:S(2)}, u32[]{:S(2)}) collective-permute-start(bf16[272,640]{1,0:T(8,128)(2,1)S(1)} %pad_maximum_fusion.1.rest_16_), channel_id=1, source_target_pairs={{0,56},{4,60},{8,0},{12,4},{16,8},{20,12},{24,16},{28,20},{32,24},... | collective-permute-start | bytes 1044488 | tf_op jit(solution)/shard_map/ppermute | solution.py:38
  8.0 0.1 convert_reduce_fusion
  8.1 0.1 convert_reduce_fusion.1
  8.2 0.1 pad_maximum_fusion.refs_0_.rest_0_.rest_8_
  8.3 1.6 %collective-permute-start = (bf16[528,640]{1,0:T(8,128)(2,1)S(1)}, bf16[528,640]{1,0:T(8,128)(2,1)S(1)}, u32[]{:S(2)}, u32[]{:S(2)}) collective-permute-start(bf16[528,640]{1,0:T(8,128)(2,1)S(1)} %pad_maximum_fusion.refs_0_.rest_0_.rest_8_), channel_id=1, source_target_pairs={{0,64},{4,68},{8,72},{12,76},{16,80},{20,84},{24,88},{28,92},{32,9... | collective-permute-start | bytes 2027528 | tf_op jit(solution)/shard_map/ppermute | solution.py:38
  9.9 1.7 %collective-permute-start.2 = (bf16[528,640]{1,0:T(8,128)(2,1)S(1)}, bf16[528,640]{1,0:T(8,128)(2,1)S(1)}, u32[]{:S(2)}, u32[]{:S(2)}) collective-permute-start(bf16[528,640]{1,0:T(8,128)(2,1)S(1)} %pad_maximum_fusion.refs_0_.rest_0_.rest_8_), channel_id=1, source_target_pairs={{0,192},{4,196},{8,200},{12,204},{16,208},{20,212},{24,216},{28,22... | collective-permute-start | bytes 2027528 | tf_op jit(solution)/shard_map/ppermute | solution.py:38
  11.6 0.0 collective-permute-start.10
  11.6 0.1 pad_add_fusion.pos_ref
  11.7 4.4 %collective-permute-done.4.rest_16_ = bf16[272,640]{1,0:T(8,128)(2,1)S(1)} collective-permute-done((bf16[272,640]{1,0:T(8,128)(2,1)S(1)}, bf16[272,640]{1,0:T(8,128)(2,1)S(1)}, u32[]{:S(2)}, u32[]{:S(2)}) %collective-permute-start.4) | collective-permute-done | bytes 348192 | tf_op jit(solution)/shard_map/ppermute | solution.py:38
  16.1 3.2 %collective-permute-start.7 = (bf16[272,640]{1,0:T(8,128)(2,1)}, bf16[272,640]{1,0:T(8,128)(2,1)S(1)}, u32[]{:S(2)}, u32[]{:S(2)}) collective-permute-start(bf16[272,640]{1,0:T(8,128)(2,1)} %collective-permute-done.5.rest_17_), channel_id=1, source_target_pairs={{0,56},{4,60},{8,0},{12,4},{16,8},{20,12},{24,16},{28,20},{32,24},... | collective-permute-start | bytes 1044488 | tf_op jit(solution)/shard_map/ppermute | solution.py:38
  19.3 0.7 constant_dynamic-update-slice_fusion.4
  20.1 6.2 %collective-permute-done.refs_6_.rest_6_.rest_14_ = bf16[528,640]{1,0:T(8,128)(2,1)S(1)} collective-permute-done((bf16[528,640]{1,0:T(8,128)(2,1)S(1)}, bf16[528,640]{1,0:T(8,128)(2,1)S(1)}, u32[]{:S(2)}, u32[]{:S(2)}) %collective-permute-start) | collective-permute-done | bytes 675872 | tf_op jit(solution)/shard_map/ppermute | solution.py:38
  26.3 0.4 collective-permute-start.1
  26.7 3.0 %collective-permute-start.3 = (bf16[256,640]{1,0:T(8,128)(2,1)S(1)}, bf16[256,640]{1,0:T(8,128)(2,1)S(1)}, u32[]{:S(2)}, u32[]{:S(2)}) collective-permute-start(bf16[256,640]{1,0:T(8,128)(2,1)S(1)} %slice.45), channel_id=1, source_target_pairs={{0,192},{4,196},{8,200},{12,204},{16,208},{20,212},{24,216},{28,22... | collective-permute-start | bytes 983048 | tf_op jit(solution)/shard_map/ppermute | solution.py:38
  29.7 0.0 collective-permute-done.7.rest_17_
  29.7 3.2 %collective-permute-start.9 = (bf16[272,640]{1,0:T(8,128)(2,1)S(1)}, bf16[272,640]{1,0:T(8,128)(2,1)S(1)}, u32[]{:S(2)}, u32[]{:S(2)}) collective-permute-start(bf16[272,640]{1,0:T(8,128)(2,1)S(1)} %collective-permute-done.7.rest_17_), channel_id=1, source_target_pairs={{0,56},{4,60},{8,0},{12,4},{16,8},{20,12},{24,16},{28,20},{32,24},... | collective-permute-start | bytes 1044488 | tf_op jit(solution)/shard_map/ppermute | solution.py:38
  32.9 6.1 %collective-permute-done.8.rest_16_.up_ref = bf16[272,640]{1,0:T(8,128)(2,1)S(1)} collective-permute-done((bf16[272,640]{1,0:T(8,128)(2,1)S(1)}, bf16[272,640]{1,0:T(8,128)(2,1)S(1)}, u32[]{:S(2)}, u32[]{:S(2)}) %collective-permute-start.8) | collective-permute-done | bytes 348192 | tf_op jit(solution)/shard_map/ppermute | solution.py:38
  39.0 0.0 collective-permute-start.11
  39.0 0.0 collective-permute-done.9.rest_17_.down_ref
  39.0 0.5 collective-permute-start.13
  39.6 0.0 collective-permute-done.3.rest_12_
  39.6 0.1 collective-permute-start.15
  39.7 3.2 %collective-permute-start.16 = (bf16[144,640]{1,0:T(8,128)(2,1)S(1)}, bf16[144,640]{1,0:T(8,128)(2,1)S(1)}, u32[]{:S(2)}, u32[]{:S(2)}) collective-permute-start(bf16[144,640]{1,0:T(8,128)(2,1)S(1)} %get-tuple-element.62), channel_id=1, source_target_pairs={{0,56},{4,60},{8,0},{12,4},{16,8},{20,12},{24,16},{28,20},{32,24},... | collective-permute-start | bytes 552968 | tf_op jit(solution)/shard_map/ppermute | solution.py:38
  42.9 3.2 %shard_map.55 = (f32[7,64,256]{2,1,0:T(8,128)S(1)}, s32[7,128]{1,0:T(8,128)S(1)}) custom-call(s32[3]{0:T(128)S(1)} %pad_add_fusion.pos_ref, bf16[112,128]{1,0:T(8,128)(2,1)S(1)} %constant_dynamic-update-slice_fusion.asked_ref), custom_call_target="tpu_custom_call" | custom-call | flops 1000000 | bytes 1048576 | tf_op jit(solution)/shard_map/pallas_call | solution.py:95
  46.1 1.3 %collective-permute-done.15.asked_ref.rest_16_ = bf16[144,640]{1,0:T(8,128)(2,1)S(1)} collective-permute-done((bf16[144,640]{1,0:T(8,128)(2,1)S(1)}, bf16[144,640]{1,0:T(8,128)(2,1)S(1)}, u32[]{:S(2)}, u32[]{:S(2)}) %collective-permute-start.15) | collective-permute-done | bytes 184352 | tf_op jit(solution)/shard_map/ppermute | solution.py:38
  47.5 0.5 collective-permute-start.14
  48.0 1.9 %shard_map.62 = (f32[1,64,256]{2,1,0:T(8,128)S(1)}, s32[2,128]{1,0:T(2,128)S(1)}) custom-call(s32[3]{0:T(128)S(1)} %pad_add_fusion.pos_ref, bf16[144,640]{1,0:T(8,128)(2,1)S(1)} %collective-permute-done.15.asked_ref.rest_16_), custom_call_target="tpu_custom_call" | custom-call | flops 1000000 | bytes 1048576 | tf_op jit(solution)/shard_map/pallas_call | solution.py:95
  49.9 0.0 collective-permute-done.11.refs_3_.rest_3_.rest_11_
  49.9 0.0 collective-permute-done.13.refs_7_.rest_7_.rest_15_
  49.9 2.0 %shard_map.63 = (bf16[672,128]{1,0:T(8,128)(2,1)S(1)}, bf16[672,128]{1,0:T(8,128)(2,1)S(1)}) custom-call(s32[2,128]{1,0:T(2,128)S(1)} %get-tuple-element.64.list_ref, bf16[64,640]{1,0:T(8,128)(2,1)S(1)} %get-tuple-element.49.mean_k_ref, bf16[64,640]{1,0:T(8,128)(2,1)S(1)} %get-tuple-element.50.mean_v_ref, f32[1,64,256]{2,1,0:T(8,128)S(1)} %get-tuple-element.65.bias_ref, ...), custom_call_target="tpu_custom_call" | custom-call | flops 1342177280 | bytes 4194304 | tf_op jit(solution)/shard_map/pallas_call | solution.py:316
  51.9 2.8 %collective-permute-start.17 = (bf16[672,128]{1,0:T(8,128)(2,1)S(1)}, bf16[672,128]{1,0:T(8,128)(2,1)S(1)}, u32[]{:S(2)}, u32[]{:S(2)}) collective-permute-start(bf16[672,128]{1,0:T(8,128)(2,1)S(1)} %get-tuple-element.67), channel_id=1, source_target_pairs={{0,56},{4,60},{8,0},{12,4},{16,8},{20,12},{24,16},{28,20},{32,24},... | collective-permute-start | bytes 516104 | tf_op jit(solution)/shard_map/ppermute | solution.py:38
  54.7 2.3 %shard_map.60 = (bf16[672,128]{1,0:T(8,128)(2,1)S(1)}, bf16[672,128]{1,0:T(8,128)(2,1)S(1)}, bf16[672,128]{1,0:T(8,128)(2,1)S(1)}, bf16[672,128]{1,0:T(8,128)(2,1)S(1)}) custom-call(s32[7,128]{1,0:T(8,128)S(1)} %get-tuple-element.47.list_ref, bf16[64,640]{1,0:T(8,128)(2,1)S(1)} %get-tuple-element.49.mean_k_ref, ...), custom_call_target="tpu_custom_call" | custom-call | flops 1342177280 | bytes 4194304 | tf_op jit(solution)/shard_map/pallas_call | solution.py:316
  57.0 3.3 %collective-permute-start.24 = (bf16[672,128]{1,0:T(8,128)(2,1)S(1)}, bf16[672,128]{1,0:T(8,128)(2,1)S(1)}, u32[]{:S(2)}, u32[]{:S(2)}) collective-permute-start(bf16[672,128]{1,0:T(8,128)(2,1)S(1)} %get-tuple-element.78), channel_id=1, source_target_pairs={{0,56},{4,60},{8,0},{12,4},{16,8},{20,12},{24,16},{28,20},{32,24},... | collective-permute-start | bytes 516104 | tf_op jit(solution)/shard_map/ppermute | solution.py:38
  60.3 2.1 %collective-permute-done.18.refs_3_ = bf16[672,128]{1,0:T(8,128)(2,1)S(1)} collective-permute-done((bf16[672,128]{1,0:T(8,128)(2,1)S(1)}, bf16[672,128]{1,0:T(8,128)(2,1)S(1)}, u32[]{:S(2)}, u32[]{:S(2)}) %collective-permute-start.18) | collective-permute-done | bytes 172064 | tf_op jit(solution)/shard_map/ppermute | solution.py:38
  62.4 0.1 shard_map.64
  62.6 1.2 %collective-permute-start.19 = (bf16[672,128]{1,0:T(8,128)(2,1)S(1)}, bf16[672,128]{1,0:T(8,128)(2,1)S(1)}, u32[]{:S(2)}, u32[]{:S(2)}) collective-permute-start(bf16[672,128]{1,0:T(8,128)(2,1)S(1)} %get-tuple-element.69), channel_id=1, source_target_pairs={{0,56},{4,60},{8,0},{12,4},{16,8},{20,12},{24,16},{28,20},{32,24},... | collective-permute-start | bytes 516104 | tf_op jit(solution)/shard_map/ppermute | solution.py:38
  63.8 0.9 collective-permute-start.20
  64.7 2.5 %shard_map.59 = (bf16[672,128]{1,0:T(8,128)(2,1)S(1)}, bf16[672,128]{1,0:T(8,128)(2,1)S(1)}, bf16[672,128]{1,0:T(8,128)(2,1)S(1)}, bf16[672,128]{1,0:T(8,128)(2,1)S(1)}) custom-call(s32[7,128]{1,0:T(8,128)S(1)} %get-tuple-element.47.list_ref, bf16[64,640]{1,0:T(8,128)(2,1)S(1)} %get-tuple-element.49.mean_k_ref, ...), custom_call_target="tpu_custom_call" | custom-call | flops 1342177280 | bytes 4194304 | tf_op jit(solution)/shard_map/pallas_call | solution.py:316
  67.2 1.0 %collective-permute-done.25.refs_3_ = bf16[672,128]{1,0:T(8,128)(2,1)S(1)} collective-permute-done((bf16[672,128]{1,0:T(8,128)(2,1)S(1)}, bf16[672,128]{1,0:T(8,128)(2,1)S(1)}, u32[]{:S(2)}, u32[]{:S(2)}) %collective-permute-start.25) | collective-permute-done | bytes 172064 | tf_op jit(solution)/shard_map/ppermute | solution.py:38
  68.2 0.2 shard_map.67
  68.3 1.4 %collective-permute-start.26 = (bf16[672,128]{1,0:T(8,128)(2,1)S(1)}, bf16[672,128]{1,0:T(8,128)(2,1)S(1)}, u32[]{:S(2)}, u32[]{:S(2)}) collective-permute-start(bf16[672,128]{1,0:T(8,128)(2,1)S(1)} %get-tuple-element.80), channel_id=1, source_target_pairs={{0,56},{4,60},{8,0},{12,4},{16,8},{20,12},{24,16},{28,20},{32,24},... | collective-permute-start | bytes 516104 | tf_op jit(solution)/shard_map/ppermute | solution.py:38
  69.8 0.7 collective-permute-start.27
  70.4 0.7 collective-permute-done.20.refs_3_
  71.2 0.1 shard_map.65
  71.3 1.9 %collective-permute-start.21 = (bf16[672,128]{1,0:T(8,128)(2,1)S(1)}, bf16[672,128]{1,0:T(8,128)(2,1)S(1)}, u32[]{:S(2)}, u32[]{:S(2)}) collective-permute-start(bf16[672,128]{1,0:T(8,128)(2,1)S(1)} %get-tuple-element.71), channel_id=1, source_target_pairs={{0,56},{4,60},{8,0},{12,4},{16,8},{20,12},{24,16},{28,20},{32,24},... | collective-permute-start | bytes 516104 | tf_op jit(solution)/shard_map/ppermute | solution.py:38
  73.3 0.2 collective-permute-start.22
  73.4 2.7 %shard_map.58 = (bf16[672,128]{1,0:T(8,128)(2,1)S(1)}, bf16[672,128]{1,0:T(8,128)(2,1)S(1)}, bf16[672,128]{1,0:T(8,128)(2,1)S(1)}, bf16[672,128]{1,0:T(8,128)(2,1)S(1)}) custom-call(s32[7,128]{1,0:T(8,128)S(1)} %get-tuple-element.47.list_ref, bf16[64,640]{1,0:T(8,128)(2,1)S(1)} %get-tuple-element.49.mean_k_ref, ...), custom_call_target="tpu_custom_call" | custom-call | flops 1342177280 | bytes 4194304 | tf_op jit(solution)/shard_map/pallas_call | solution.py:316
  76.1 1.7 %collective-permute-done.27.refs_3_ = bf16[672,128]{1,0:T(8,128)(2,1)S(1)} collective-permute-done((bf16[672,128]{1,0:T(8,128)(2,1)S(1)}, bf16[672,128]{1,0:T(8,128)(2,1)S(1)}, u32[]{:S(2)}, u32[]{:S(2)}) %collective-permute-start.27) | collective-permute-done | bytes 172064 | tf_op jit(solution)/shard_map/ppermute | solution.py:38
  77.8 0.2 shard_map.68
  78.0 1.5 %collective-permute-start.28 = (bf16[672,128]{1,0:T(8,128)(2,1)S(1)}, bf16[672,128]{1,0:T(8,128)(2,1)S(1)}, u32[]{:S(2)}, u32[]{:S(2)}) collective-permute-start(bf16[672,128]{1,0:T(8,128)(2,1)S(1)} %get-tuple-element.82), channel_id=1, source_target_pairs={{0,56},{4,60},{8,0},{12,4},{16,8},{20,12},{24,16},{28,20},{32,24},... | collective-permute-start | bytes 516104 | tf_op jit(solution)/shard_map/ppermute | solution.py:38
  79.4 0.7 collective-permute-start.29
  80.1 0.1 shard_map.66
  80.3 2.6 %collective-permute-start.23 = (bf16[672,128]{1,0:T(8,128)(2,1)S(1)}, bf16[672,128]{1,0:T(8,128)(2,1)S(1)}, u32[]{:S(2)}, u32[]{:S(2)}) collective-permute-start(bf16[672,128]{1,0:T(8,128)(2,1)S(1)} %get-tuple-element.73), channel_id=1, source_target_pairs={{0,56},{4,60},{8,0},{12,4},{16,8},{20,12},{24,16},{28,20},{32,24},... | collective-permute-start | bytes 516104 | tf_op jit(solution)/shard_map/ppermute | solution.py:38
  82.9 1.5 %shard_map.57 = (bf16[672,128]{1,0:T(8,128)(2,1)S(1)}, bf16[672,128]{1,0:T(8,128)(2,1)S(1)}) custom-call(s32[7,128]{1,0:T(8,128)S(1)} %get-tuple-element.47.list_ref, bf16[64,640]{1,0:T(8,128)(2,1)S(1)} %get-tuple-element.49.mean_k_ref, bf16[64,640]{1,0:T(8,128)(2,1)S(1)} %get-tuple-element.50.mean_v_ref, f32[7,64,256]{2,1,0:T(8,128)S(1)} %get-tuple-element.51.bias_ref, ...), custom_call_target="tpu_custom_call" | custom-call | flops 1342177280 | bytes 4194304 | tf_op jit(solution)/shard_map/pallas_call | solution.py:316
  84.4 0.6 collective-permute-done.28.refs_3_
  85.0 2.2 %collective-permute-done.29.refs_4_ = bf16[672,128]{1,0:T(8,128)(2,1)S(1)} collective-permute-done((bf16[672,128]{1,0:T(8,128)(2,1)S(1)}, bf16[672,128]{1,0:T(8,128)(2,1)S(1)}, u32[]{:S(2)}, u32[]{:S(2)}) %collective-permute-start.29) | collective-permute-done | bytes 172064 | tf_op jit(solution)/shard_map/ppermute | solution.py:38
  87.3 2.3 %collective-permute-done.30.refs_5_ = bf16[672,128]{1,0:T(8,128)(2,1)S(1)} collective-permute-done((bf16[672,128]{1,0:T(8,128)(2,1)S(1)}, bf16[672,128]{1,0:T(8,128)(2,1)S(1)}, u32[]{:S(2)}, u32[]{:S(2)}) %collective-permute-start.30) | collective-permute-done | bytes 172064 | tf_op jit(solution)/shard_map/ppermute | solution.py:38
  89.5 1.0 %shard_map.69 = bf16[256,640]{1,0:T(8,128)(2,1)} custom-call(bf16[672,128]{1,0:T(8,128)(2,1)S(1)} %get-tuple-element.53.refs_0_, bf16[672,128]{1,0:T(8,128)(2,1)S(1)} %get-tuple-element.54.refs_1_, bf16[672,128]{1,0:T(8,128)(2,1)S(1)} %collective-permute-done.23.refs_2_, bf16[672,128]{1,0:T(8,128)(2,1)S(1)} %collective-permute-done.28.refs_3_, ...), custom_call_target="tpu_custom_call" | custom-call | tf_op jit(solution)/shard_map/pallas_call | solution.py:380
  (37 shorter events, 0.3 us)
Async XLA Ops:
  0.9 7.2 %copy-start = (bf16[256,640]{1,0:T(8,128)(2,1)S(1)}, bf16[256,640]{1,0:T(8,128)(2,1)}, u32[]{:S(2)}) copy-start(bf16[256,640]{1,0:T(8,128)(2,1)} %param.7) | copy-start | bytes 983044
  2.0 6.2 %copy-start.1 = (bf16[256,640]{1,0:T(8,128)(2,1)S(1)}, bf16[256,640]{1,0:T(8,128)(2,1)}, u32[]{:S(2)}) copy-start(bf16[256,640]{1,0:T(8,128)(2,1)} %param.6) | copy-start | bytes 983044
  2.0 14.1 %collective-permute-start.4 = (bf16[272,640]{1,0:T(8,128)(2,1)S(1)}, bf16[272,640]{1,0:T(8,128)(2,1)S(1)}, u32[]{:S(2)}, u32[]{:S(2)}) collective-permute-start(bf16[272,640]{1,0:T(8,128)(2,1)S(1)} %pad_maximum_fusion.1.rest_16_), channel_id=1, source_target_pairs={{0,8},{4,12},{8,16},{12,20},{16,24},{20,28},{24,32},{28,36},{32,40... | collective-permute-start | bytes 1044488 | tf_op jit(solution)/shard_map/ppermute | solution.py:38
  4.0 12.1 %collective-permute-start.5 = (bf16[272,640]{1,0:T(8,128)(2,1)S(1)}, bf16[272,640]{1,0:T(8,128)(2,1)}, u32[]{:S(2)}, u32[]{:S(2)}) collective-permute-start(bf16[272,640]{1,0:T(8,128)(2,1)S(1)} %pad_maximum_fusion.1.rest_16_), channel_id=1, source_target_pairs={{0,56},{4,60},{8,0},{12,4},{16,8},{20,12},{24,16},{28,20},{32,24},... | collective-permute-start | bytes 1044488 | tf_op jit(solution)/shard_map/ppermute | solution.py:38
  8.3 17.9 %collective-permute-start = (bf16[528,640]{1,0:T(8,128)(2,1)S(1)}, bf16[528,640]{1,0:T(8,128)(2,1)S(1)}, u32[]{:S(2)}, u32[]{:S(2)}) collective-permute-start(bf16[528,640]{1,0:T(8,128)(2,1)S(1)} %pad_maximum_fusion.refs_0_.rest_0_.rest_8_), channel_id=1, source_target_pairs={{0,64},{4,68},{8,72},{12,76},{16,80},{20,84},{24,88},{28,92},{32,9... | collective-permute-start | bytes 2027528 | tf_op jit(solution)/shard_map/ppermute | solution.py:38
  9.9 16.7 %collective-permute-start.2 = (bf16[528,640]{1,0:T(8,128)(2,1)S(1)}, bf16[528,640]{1,0:T(8,128)(2,1)S(1)}, u32[]{:S(2)}, u32[]{:S(2)}) collective-permute-start(bf16[528,640]{1,0:T(8,128)(2,1)S(1)} %pad_maximum_fusion.refs_0_.rest_0_.rest_8_), channel_id=1, source_target_pairs={{0,192},{4,196},{8,200},{12,204},{16,208},{20,212},{24,216},{28,22... | collective-permute-start | bytes 2027528 | tf_op jit(solution)/shard_map/ppermute | solution.py:38
  11.6 38.2 %collective-permute-start.10 = (bf16[528,640]{1,0:T(8,128)(2,1)S(1)}, bf16[528,640]{1,0:T(8,128)(2,1)S(1)}, u32[]{:S(2)}, u32[]{:S(2)}) collective-permute-start(bf16[528,640]{1,0:T(8,128)(2,1)S(1)} %pad_maximum_fusion.refs_0_.rest_0_.rest_8_), channel_id=1, source_target_pairs={{0,4},{4,0},{8,12},{12,8},{16,20},{20,16},{24,28},{28,24},{32,36},... | collective-permute-start | bytes 2027528 | tf_op jit(solution)/shard_map/ppermute | solution.py:38
  16.1 13.6 %collective-permute-start.6 = (bf16[272,640]{1,0:T(8,128)(2,1)S(1)}, bf16[272,640]{1,0:T(8,128)(2,1)S(1)}, u32[]{:S(2)}, u32[]{:S(2)}) collective-permute-start(bf16[272,640]{1,0:T(8,128)(2,1)S(1)} %collective-permute-done.4.rest_16_), channel_id=1, source_target_pairs={{0,8},{4,12},{8,16},{12,20},{16,24},{20,28},{24,32},{28,36},{32,40... | collective-permute-start | bytes 1044488 | tf_op jit(solution)/shard_map/ppermute | solution.py:38
  16.1 13.6 %collective-permute-start.7 = (bf16[272,640]{1,0:T(8,128)(2,1)}, bf16[272,640]{1,0:T(8,128)(2,1)S(1)}, u32[]{:S(2)}, u32[]{:S(2)}) collective-permute-start(bf16[272,640]{1,0:T(8,128)(2,1)} %collective-permute-done.5.rest_17_), channel_id=1, source_target_pairs={{0,56},{4,60},{8,0},{12,4},{16,8},{20,12},{24,16},{28,20},{32,24},... | collective-permute-start | bytes 1044488 | tf_op jit(solution)/shard_map/ppermute | solution.py:38
  26.3 13.4 %collective-permute-start.1 = (bf16[272,640]{1,0:T(8,128)(2,1)S(1)}, bf16[272,640]{1,0:T(8,128)(2,1)S(1)}, u32[]{:S(2)}, u32[]{:S(2)}) collective-permute-start(bf16[272,640]{1,0:T(8,128)(2,1)S(1)} %slice.44), channel_id=1, source_target_pairs={{0,64},{4,68},{8,72},{12,76},{16,80},{20,84},{24,88},{28,92},{32,9... | collective-permute-start | bytes 1044488 | tf_op jit(solution)/shard_map/ppermute | solution.py:38
  26.7 12.9 %collective-permute-start.3 = (bf16[256,640]{1,0:T(8,128)(2,1)S(1)}, bf16[256,640]{1,0:T(8,128)(2,1)S(1)}, u32[]{:S(2)}, u32[]{:S(2)}) collective-permute-start(bf16[256,640]{1,0:T(8,128)(2,1)S(1)} %slice.45), channel_id=1, source_target_pairs={{0,192},{4,196},{8,200},{12,204},{16,208},{20,212},{24,216},{28,22... | collective-permute-start | bytes 983048 | tf_op jit(solution)/shard_map/ppermute | solution.py:38
  29.7 9.4 %collective-permute-start.8 = (bf16[272,640]{1,0:T(8,128)(2,1)S(1)}, bf16[272,640]{1,0:T(8,128)(2,1)S(1)}, u32[]{:S(2)}, u32[]{:S(2)}) collective-permute-start(bf16[272,640]{1,0:T(8,128)(2,1)S(1)} %collective-permute-done.6.rest_16_), channel_id=1, source_target_pairs={{0,8},{4,12},{8,16},{12,20},{16,24},{20,28},{24,32},{28,36},{32,40... | collective-permute-start | bytes 1044488 | tf_op jit(solution)/shard_map/ppermute | solution.py:38
  29.7 9.3 %collective-permute-start.9 = (bf16[272,640]{1,0:T(8,128)(2,1)S(1)}, bf16[272,640]{1,0:T(8,128)(2,1)S(1)}, u32[]{:S(2)}, u32[]{:S(2)}) collective-permute-start(bf16[272,640]{1,0:T(8,128)(2,1)S(1)} %collective-permute-done.7.rest_17_), channel_id=1, source_target_pairs={{0,56},{4,60},{8,0},{12,4},{16,8},{20,12},{24,16},{28,20},{32,24},... | collective-permute-start | bytes 1044488 | tf_op jit(solution)/shard_map/ppermute | solution.py:38
  39.0 10.8 %collective-permute-start.11 = (bf16[528,640]{1,0:T(8,128)(2,1)S(1)}, bf16[528,640]{1,0:T(8,128)(2,1)S(1)}, u32[]{:S(2)}, u32[]{:S(2)}) collective-permute-start(bf16[528,640]{1,0:T(8,128)(2,1)S(1)} %collective-permute-done.2.refs_2_.rest_2_.rest_10_), channel_id=1, source_target_pairs={{0,4},{4,0},{8,12},{12,8},{16,20},{20,16},{24,28},{28,24},{32,36},... | collective-permute-start | bytes 2027528 | tf_op jit(solution)/shard_map/ppermute | solution.py:38
  39.0 10.8 %collective-permute-start.13 = (bf16[528,640]{1,0:T(8,128)(2,1)S(1)}, bf16[528,640]{1,0:T(8,128)(2,1)S(1)}, u32[]{:S(2)}, u32[]{:S(2)}) collective-permute-start(bf16[528,640]{1,0:T(8,128)(2,1)S(1)} %collective-permute-done.refs_6_.rest_6_.rest_14_), channel_id=1, source_target_pairs={{0,4},{4,0},{8,12},{12,8},{16,20},{20,16},{24,28},{28,24},{32,36},... | collective-permute-start | bytes 2027528 | tf_op jit(solution)/shard_map/ppermute | solution.py:38
  39.6 7.8 %collective-permute-start.15 = (bf16[144,640]{1,0:T(8,128)(2,1)S(1)}, bf16[144,640]{1,0:T(8,128)(2,1)S(1)}, u32[]{:S(2)}, u32[]{:S(2)}) collective-permute-start(bf16[144,640]{1,0:T(8,128)(2,1)S(1)} %get-tuple-element.61), channel_id=1, source_target_pairs={{0,8},{4,12},{8,16},{12,20},{16,24},{20,28},{24,32},{28,36},{32,40... | collective-permute-start | bytes 552968 | tf_op jit(solution)/shard_map/ppermute | solution.py:38
  39.7 7.7 %collective-permute-start.16 = (bf16[144,640]{1,0:T(8,128)(2,1)S(1)}, bf16[144,640]{1,0:T(8,128)(2,1)S(1)}, u32[]{:S(2)}, u32[]{:S(2)}) collective-permute-start(bf16[144,640]{1,0:T(8,128)(2,1)S(1)} %get-tuple-element.62), channel_id=1, source_target_pairs={{0,56},{4,60},{8,0},{12,4},{16,8},{20,12},{24,16},{28,20},{32,24},... | collective-permute-start | bytes 552968 | tf_op jit(solution)/shard_map/ppermute | solution.py:38
  47.4 2.5 %collective-permute-start.12 = (bf16[272,640]{1,0:T(8,128)(2,1)S(1)}, bf16[272,640]{1,0:T(8,128)(2,1)S(1)}, u32[]{:S(2)}, u32[]{:S(2)}) collective-permute-start(bf16[272,640]{1,0:T(8,128)(2,1)S(1)} %collective-permute-done.1.refs_4_.rest_4_), channel_id=1, source_target_pairs={{0,4},{4,0},{8,12},{12,8},{16,20},{20,16},{24,28},{28,24},{32,36},... | collective-permute-start | bytes 1044488 | tf_op jit(solution)/shard_map/ppermute | solution.py:38
  47.5 2.5 %collective-permute-start.14 = (bf16[256,640]{1,0:T(8,128)(2,1)S(1)}, bf16[256,640]{1,0:T(8,128)(2,1)S(1)}, u32[]{:S(2)}, u32[]{:S(2)}) collective-permute-start(bf16[256,640]{1,0:T(8,128)(2,1)S(1)} %collective-permute-done.3.rest_12_), channel_id=1, source_target_pairs={{0,4},{4,0},{8,12},{12,8},{16,20},{20,16},{24,28},{28,24},{32,36},... | collective-permute-start | bytes 983048 | tf_op jit(solution)/shard_map/ppermute | solution.py:38
  51.9 8.4 %collective-permute-start.17 = (bf16[672,128]{1,0:T(8,128)(2,1)S(1)}, bf16[672,128]{1,0:T(8,128)(2,1)S(1)}, u32[]{:S(2)}, u32[]{:S(2)}) collective-permute-start(bf16[672,128]{1,0:T(8,128)(2,1)S(1)} %get-tuple-element.67), channel_id=1, source_target_pairs={{0,56},{4,60},{8,0},{12,4},{16,8},{20,12},{24,16},{28,20},{32,24},... | collective-permute-start | bytes 516104 | tf_op jit(solution)/shard_map/ppermute | solution.py:38
  54.7 7.7 %collective-permute-start.18 = (bf16[672,128]{1,0:T(8,128)(2,1)S(1)}, bf16[672,128]{1,0:T(8,128)(2,1)S(1)}, u32[]{:S(2)}, u32[]{:S(2)}) collective-permute-start(bf16[672,128]{1,0:T(8,128)(2,1)S(1)} %get-tuple-element.68), channel_id=1, source_target_pairs={{0,8},{4,12},{8,16},{12,20},{16,24},{20,28},{24,32},{28,36},{32,40... | collective-permute-start | bytes 516104 | tf_op jit(solution)/shard_map/ppermute | solution.py:38
  57.0 10.2 %collective-permute-start.24 = (bf16[672,128]{1,0:T(8,128)(2,1)S(1)}, bf16[672,128]{1,0:T(8,128)(2,1)S(1)}, u32[]{:S(2)}, u32[]{:S(2)}) collective-permute-start(bf16[672,128]{1,0:T(8,128)(2,1)S(1)} %get-tuple-element.78), channel_id=1, source_target_pairs={{0,56},{4,60},{8,0},{12,4},{16,8},{20,12},{24,16},{28,20},{32,24},... | collective-permute-start | bytes 516104 | tf_op jit(solution)/shard_map/ppermute | solution.py:38
  60.3 7.9 %collective-permute-start.25 = (bf16[672,128]{1,0:T(8,128)(2,1)S(1)}, bf16[672,128]{1,0:T(8,128)(2,1)S(1)}, u32[]{:S(2)}, u32[]{:S(2)}) collective-permute-start(bf16[672,128]{1,0:T(8,128)(2,1)S(1)} %get-tuple-element.79), channel_id=1, source_target_pairs={{0,8},{4,12},{8,16},{12,20},{16,24},{20,28},{24,32},{28,36},{32,40... | collective-permute-start | bytes 516104 | tf_op jit(solution)/shard_map/ppermute | solution.py:38
  62.6 7.9 %collective-permute-start.19 = (bf16[672,128]{1,0:T(8,128)(2,1)S(1)}, bf16[672,128]{1,0:T(8,128)(2,1)S(1)}, u32[]{:S(2)}, u32[]{:S(2)}) collective-permute-start(bf16[672,128]{1,0:T(8,128)(2,1)S(1)} %get-tuple-element.69), channel_id=1, source_target_pairs={{0,56},{4,60},{8,0},{12,4},{16,8},{20,12},{24,16},{28,20},{32,24},... | collective-permute-start | bytes 516104 | tf_op jit(solution)/shard_map/ppermute | solution.py:38
  63.8 7.4 %collective-permute-start.20 = (bf16[672,128]{1,0:T(8,128)(2,1)S(1)}, bf16[672,128]{1,0:T(8,128)(2,1)S(1)}, u32[]{:S(2)}, u32[]{:S(2)}) collective-permute-start(bf16[672,128]{1,0:T(8,128)(2,1)S(1)} %get-tuple-element.70), channel_id=1, source_target_pairs={{0,8},{4,12},{8,16},{12,20},{16,24},{20,28},{24,32},{28,36},{32,40... | collective-permute-start | bytes 516104 | tf_op jit(solution)/shard_map/ppermute | solution.py:38
  68.3 7.8 %collective-permute-start.26 = (bf16[672,128]{1,0:T(8,128)(2,1)S(1)}, bf16[672,128]{1,0:T(8,128)(2,1)S(1)}, u32[]{:S(2)}, u32[]{:S(2)}) collective-permute-start(bf16[672,128]{1,0:T(8,128)(2,1)S(1)} %get-tuple-element.80), channel_id=1, source_target_pairs={{0,56},{4,60},{8,0},{12,4},{16,8},{20,12},{24,16},{28,20},{32,24},... | collective-permute-start | bytes 516104 | tf_op jit(solution)/shard_map/ppermute | solution.py:38
  69.8 8.0 %collective-permute-start.27 = (bf16[672,128]{1,0:T(8,128)(2,1)S(1)}, bf16[672,128]{1,0:T(8,128)(2,1)S(1)}, u32[]{:S(2)}, u32[]{:S(2)}) collective-permute-start(bf16[672,128]{1,0:T(8,128)(2,1)S(1)} %get-tuple-element.81), channel_id=1, source_target_pairs={{0,8},{4,12},{8,16},{12,20},{16,24},{20,28},{24,32},{28,36},{32,40... | collective-permute-start | bytes 516104 | tf_op jit(solution)/shard_map/ppermute | solution.py:38
  71.3 8.8 %collective-permute-start.21 = (bf16[672,128]{1,0:T(8,128)(2,1)S(1)}, bf16[672,128]{1,0:T(8,128)(2,1)S(1)}, u32[]{:S(2)}, u32[]{:S(2)}) collective-permute-start(bf16[672,128]{1,0:T(8,128)(2,1)S(1)} %get-tuple-element.71), channel_id=1, source_target_pairs={{0,56},{4,60},{8,0},{12,4},{16,8},{20,12},{24,16},{28,20},{32,24},... | collective-permute-start | bytes 516104 | tf_op jit(solution)/shard_map/ppermute | solution.py:38
  73.3 6.9 %collective-permute-start.22 = (bf16[672,128]{1,0:T(8,128)(2,1)S(1)}, bf16[672,128]{1,0:T(8,128)(2,1)S(1)}, u32[]{:S(2)}, u32[]{:S(2)}) collective-permute-start(bf16[672,128]{1,0:T(8,128)(2,1)S(1)} %get-tuple-element.72), channel_id=1, source_target_pairs={{0,8},{4,12},{8,16},{12,20},{16,24},{20,28},{24,32},{28,36},{32,40... | collective-permute-start | bytes 516104 | tf_op jit(solution)/shard_map/ppermute | solution.py:38
  78.0 7.0 %collective-permute-start.28 = (bf16[672,128]{1,0:T(8,128)(2,1)S(1)}, bf16[672,128]{1,0:T(8,128)(2,1)S(1)}, u32[]{:S(2)}, u32[]{:S(2)}) collective-permute-start(bf16[672,128]{1,0:T(8,128)(2,1)S(1)} %get-tuple-element.82), channel_id=1, source_target_pairs={{0,56},{4,60},{8,0},{12,4},{16,8},{20,12},{24,16},{28,20},{32,24},... | collective-permute-start | bytes 516104 | tf_op jit(solution)/shard_map/ppermute | solution.py:38
  79.4 7.8 %collective-permute-start.29 = (bf16[672,128]{1,0:T(8,128)(2,1)S(1)}, bf16[672,128]{1,0:T(8,128)(2,1)S(1)}, u32[]{:S(2)}, u32[]{:S(2)}) collective-permute-start(bf16[672,128]{1,0:T(8,128)(2,1)S(1)} %get-tuple-element.83), channel_id=1, source_target_pairs={{0,8},{4,12},{8,16},{12,20},{16,24},{20,28},{24,32},{28,36},{32,40... | collective-permute-start | bytes 516104 | tf_op jit(solution)/shard_map/ppermute | solution.py:38
  80.3 7.0 %collective-permute-start.23 = (bf16[672,128]{1,0:T(8,128)(2,1)S(1)}, bf16[672,128]{1,0:T(8,128)(2,1)S(1)}, u32[]{:S(2)}, u32[]{:S(2)}) collective-permute-start(bf16[672,128]{1,0:T(8,128)(2,1)S(1)} %get-tuple-element.73), channel_id=1, source_target_pairs={{0,56},{4,60},{8,0},{12,4},{16,8},{20,12},{24,16},{28,20},{32,24},... | collective-permute-start | bytes 516104 | tf_op jit(solution)/shard_map/ppermute | solution.py:38
  82.9 6.6 %collective-permute-start.30 = (bf16[672,128]{1,0:T(8,128)(2,1)S(1)}, bf16[672,128]{1,0:T(8,128)(2,1)S(1)}, u32[]{:S(2)}, u32[]{:S(2)}) collective-permute-start(bf16[672,128]{1,0:T(8,128)(2,1)S(1)} %get-tuple-element.84), channel_id=1, source_target_pairs={{0,8},{4,12},{8,16},{12,20},{16,24},{20,28},{24,32},{28,36},{32,40... | collective-permute-start | bytes 516104 | tf_op jit(solution)/shard_map/ppermute | solution.py:38
